TPU v7x, 32 devices: a whole 2x2x4 slice. The times are simulated.
32 devices in a mesh: crop: 2 (over y), row: 16 (over z, x, core).
Axes of the slice: x: 2, y: 2, z: 4, core: 2. Of those that a mesh axis runs over, the one named last changes fastest.
Arguments:
- pair: float32 [2, 64, 64, 128], P('crop', 'row'), may hold values from -6 to 6
- bins: int32 [2, 64, 64], P('crop', 'row'), may hold values from 0 to 63
- lengths: int32 [2], P('crop'), may hold values from 32 to 64, as said below
- mats: float32 [11, 128, 128], replicated, may hold values from -0.5 to 0.5
- mats_m: float32 [11, 128, 128], replicated, may hold values from -0.0010095568 to 0.0010095568
- mats_v: float32 [11, 128, 128], replicated, may hold values from 2.7901785e-07 to 1.1055424e-06
- pbias: float32 [128, 4], replicated, may hold values from -0.5 to 0.5
- pbias_m: float32 [128, 4], replicated, may hold values from -0.0010095568 to 0.0010095568
- pbias_v: float32 [128, 4], replicated, may hold values from 1.0528976e-08 to 4.2115904e-08
- head: float32 [128, 64], replicated, may hold values from -0.5 to 0.5
- head_m: float32 [128, 64], replicated, may hold values from -0.0010095568 to 0.0010095568
- head_v: float32 [128, 64], replicated, may hold values from 2.7901785e-07 to 1.1055424e-06
- norms: float32 [8, 128], replicated, may hold values from 0.5 to 1.5
- norms_m: float32 [8, 128], replicated, may hold values from -0.0010095568 to 0.0010095568
- norms_v: float32 [8, 128], replicated, may hold values from 2.7901785e-07 to 1.1055424e-06
Outputs:
- grad_norm: float32 [], replicated
- loss_sum: float32 [], replicated
- loss_count: float32 [], replicated
- mats_m_new: float32 [11, 128, 128], replicated
- mats_v_new: float32 [11, 128, 128], replicated
- mats_new: float32 [11, 128, 128], replicated
- mats_low: bfloat16 [11, 128, 128], replicated
- pbias_m_new: float32 [128, 4], replicated
- pbias_v_new: float32 [128, 4], replicated
- pbias_new: float32 [128, 4], replicated
- head_m_new: float32 [128, 64], replicated
- head_v_new: float32 [128, 64], replicated
- head_new: float32 [128, 64], replicated
- norms_m_new: float32 [8, 128], replicated
- norms_v_new: float32 [8, 128], replicated
- norms_new: float32 [8, 128], replicated
Inputs may be any that keep to these rules, and one draw needn't show every extreme that they name: `lengths`: each crop's length lies between 32 and 64; in every draw some crop, drawn from the seed, has length 64.
All inputs are finite; a program needn't handle non-finite values.
Results may differ from a plain program's by a relative error of at most 0.0024.
The roundings to bfloat16 on the way count: a program that leaves them out, or rounds other values in their place, can miss the bound.
Values may be sent and summed in bfloat16 or wider, within the bound.
No kernel may reach another device: no remote copies, remote signals or barrier semaphores. Data moves between devices by JAX's collectives and lax.ppermute only.
A program may use at most 512 MiB of HBM per device.

v0:
```python
import functools

import jax
import jax.numpy as jnp
from jax import lax
from jax.experimental import pallas as pl
from jax.experimental.pallas import tpu as pltpu
from jax.sharding import PartitionSpec as P

STEP = 5


EPS_NORM = 1e-05
CLIP = 1.0
RATE = 0.05
BETA1 = 0.9
BETA2 = 0.95
ADAM_EPS = 1e-08
WDECAY = 0.01


def norm_fwd(v, gain, shift):
    mean = jnp.mean(v, axis=-1, keepdims=True)
    cent = v - mean
    rstd = lax.rsqrt(jnp.mean(cent * cent, axis=-1, keepdims=True) + EPS_NORM)
    unit = cent * rstd
    return (unit * gain + shift, unit, rstd)


def norm_back(grad, unit, rstd, gain):
    dgain = jnp.sum(grad * unit, axis=(0, 1))
    dshift = jnp.sum(grad, axis=(0, 1))
    dunit = grad * gain
    dval = rstd * (
        dunit
        - jnp.mean(dunit, axis=-1, keepdims=True)
        - unit * jnp.mean(dunit * unit, axis=-1, keepdims=True)
    )
    return (dval, dgain, dshift)


def matmul(value, weight):
    flat = value.reshape(-1, value.shape[-1])
    out = jnp.dot(flat, weight, preferred_element_type=jnp.float32)
    return out.reshape(value.shape[:-1] + (weight.shape[1],))


def wgrad(value, grad):
    return jnp.einsum("ijc,ijd->cd", value, grad, preferred_element_type=jnp.float32)


def adam(weight, grad, first, second):
    first_new = BETA1 * first + (1.0 - BETA1) * grad
    second_new = BETA2 * second + (1.0 - BETA2) * grad * grad
    m_hat = first_new / (1.0 - BETA1**STEP)
    v_hat = second_new / (1.0 - BETA2**STEP)
    weight_new = weight - RATE * (m_hat / (jnp.sqrt(v_hat) + ADAM_EPS) + WDECAY * weight)
    return (first_new, second_new, weight_new)


def general_step(
    pair,
    bins,
    lengths,
    mats,
    mats_m,
    mats_v,
    pbias,
    pbias_m,
    pbias_v,
    head,
    head_m,
    head_v,
    norms,
    norms_m,
    norms_v,
):
    bf = jnp.bfloat16
    fl = jnp.float32
    width = mats.shape[1]
    rows = pair.shape[1]
    cols = pair.shape[2]
    heads = pbias.shape[1]
    size_head = width // heads
    scale = size_head ** (-0.5)
    start_pair = pair[0]
    first_row = lax.axis_index("row") * rows
    limit = lengths[0]
    row_ok = first_row + jnp.arange(rows) < limit
    col_ok = jnp.arange(cols) < limit
    pmask = (row_ok[:, None] & col_ok[None, :]).astype(fl)
    m3 = pmask[..., None]
    wl = mats.astype(bf)
    pl = pbias.astype(bf)
    hl = head.astype(bf)
    w_tri = jnp.concatenate([wl[0], wl[1], wl[2], wl[3], wl[4]], axis=1)
    w_att = jnp.concatenate([wl[6], wl[7], wl[8], wl[9]], axis=1)
    h0, unit0, rstd0 = norm_fwd(start_pair, norms[0], norms[1])
    h0b = h0.astype(bf)
    proj = matmul(h0b, w_tri)
    sig_a = jax.nn.sigmoid(proj[..., width : 2 * width])
    sig_b = jax.nn.sigmoid(proj[..., 3 * width : 4 * width])
    gate = jax.nn.sigmoid(proj[..., 4 * width :])
    a_low = (sig_a * proj[..., :width] * m3).astype(bf)
    b_low = (sig_b * proj[..., 2 * width : 3 * width] * m3).astype(bf)
    b_all = lax.all_gather(b_low, "row", axis=0, tiled=True)
    prod = jnp.einsum("ikc,jkc->ijc", a_low, b_all, preferred_element_type=fl)
    y_val, unit2, rstd2 = norm_fwd(prod, norms[2], norms[3])
    y_low = y_val.astype(bf)
    out1 = matmul(y_low, wl[5])
    z1 = start_pair + gate * out1
    h1, unit4, rstd4 = norm_fwd(z1, norms[4], norms[5])
    h1b = h1.astype(bf)
    qkvg = matmul(h1b, w_att)
    query = qkvg[..., :width].astype(bf).reshape(rows, cols, heads, size_head)
    keys = qkvg[..., width : 2 * width].astype(bf).reshape(rows, cols, heads, size_head)
    values = qkvg[..., 2 * width : 3 * width].astype(bf).reshape(rows, cols, heads, size_head)
    gate2 = jax.nn.sigmoid(qkvg[..., 3 * width :])
    tb_low = matmul(h1b, pl).astype(bf)
    tb_all = lax.all_gather(tb_low, "row", axis=0, tiled=True)
    tb_heads = jnp.transpose(tb_all, (2, 0, 1)).astype(fl)
    scores = (
        jnp.einsum("ijhd,ikhd->ihjk", query, keys, preferred_element_type=fl) * scale
        + tb_heads[None]
    )
    scores = jnp.where(col_ok[None, None, None, :], scores, -1000000000.0)
    probs = jax.nn.softmax(scores, axis=-1)
    p_low = probs.astype(bf)
    att = jnp.einsum("ihjk,ikhd->ijhd", p_low, values, preferred_element_type=fl).reshape(
        rows, cols, width
    )
    u_low = (gate2 * att).astype(bf)
    z2 = z1 + matmul(u_low, wl[10])
    h2, unit6, rstd6 = norm_fwd(z2, norms[6], norms[7])
    h2b = h2.astype(bf)
    logits = matmul(h2b, hl)
    lse = jax.nn.logsumexp(logits, axis=-1)
    onehot = (bins[0][..., None] == jnp.arange(logits.shape[-1])).astype(fl)
    pick = jnp.sum(logits * onehot, axis=-1)
    loss = jnp.sum(pmask * (lse - pick))
    count = jnp.sum(pmask)
    dlog = (m3 * (jnp.exp(logits - lse[..., None]) - onehot)).astype(bf)
    dhead = wgrad(h2b, dlog)
    dz2, dg6, ds6 = norm_back(matmul(dlog, hl.T), unit6, rstd6, norms[6])
    dout2 = dz2.astype(bf)
    dw10 = wgrad(u_low, dout2)
    du = matmul(dout2, wl[10].T)
    dgate2 = du * att
    datt = (du * gate2).astype(bf).reshape(rows, cols, heads, size_head)
    dprob = jnp.einsum("ijhd,ikhd->ihjk", datt, values, preferred_element_type=fl)
    dvals = jnp.einsum("ihjk,ijhd->ikhd", p_low, datt, preferred_element_type=fl)
    dscore = (probs * (dprob - jnp.sum(dprob * probs, axis=-1, keepdims=True))).astype(bf)
    dquery = jnp.einsum("ihjk,ikhd->ijhd", dscore, keys, preferred_element_type=fl) * scale
    dkeys = jnp.einsum("ihjk,ijhd->ikhd", dscore, query, preferred_element_type=fl) * scale
    dtb = jnp.sum(dscore.astype(fl), axis=0)
    dtb_own = lax.psum_scatter(dtb, "row", scatter_dimension=1, tiled=True)
    dtb_low = jnp.transpose(dtb_own, (1, 2, 0)).astype(bf)
    dpbias = wgrad(h1b, dtb_low)
    dqkvg = jnp.concatenate(
        [
            dquery.reshape(rows, cols, width),
            dkeys.reshape(rows, cols, width),
            dvals.reshape(rows, cols, width),
            dgate2 * gate2 * (1.0 - gate2),
        ],
        axis=-1,
    ).astype(bf)
    dw_att = wgrad(h1b, dqkvg)
    dh1 = matmul(dqkvg, w_att.T) + matmul(dtb_low, pl.T)
    dn4, dg4, ds4 = norm_back(dh1, unit4, rstd4, norms[4])
    dz1 = dz2 + dn4
    dout1 = (dz1 * gate).astype(bf)
    dw5 = wgrad(y_low, dout1)
    dgate = dz1 * out1
    dxn, dg2, ds2 = norm_back(matmul(dout1, wl[5].T), unit2, rstd2, norms[2])
    dx_low = dxn.astype(bf)
    dside_a = jnp.einsum("ijc,jkc->ikc", dx_low, b_all, preferred_element_type=fl)
    dside_b = lax.psum_scatter(
        jnp.einsum("ijc,ikc->jkc", dx_low, a_low, preferred_element_type=fl),
        "row",
        scatter_dimension=0,
        tiled=True,
    )
    da_r = dside_a.astype(bf).astype(fl)
    db_r = dside_b.astype(bf).astype(fl)
    dproj = jnp.concatenate(
        [
            da_r * sig_a * m3,
            da_r * proj[..., :width] * m3 * sig_a * (1.0 - sig_a),
            db_r * sig_b * m3,
            db_r * proj[..., 2 * width : 3 * width] * m3 * sig_b * (1.0 - sig_b),
            dgate * gate * (1.0 - gate),
        ],
        axis=-1,
    ).astype(bf)
    dw_tri = wgrad(h0b, dproj)
    dh0 = matmul(dproj, w_tri.T)
    unused, dg0, ds0 = norm_back(dh0, unit0, rstd0, norms[0])
    pieces = [dw_tri[:, idx * width : (idx + 1) * width] for idx in range(5)]
    pieces = (
        pieces + [dw5] + [dw_att[:, idx * width : (idx + 1) * width] for idx in range(4)] + [dw10]
    )
    dmats = jnp.stack(pieces)
    dnorms = jnp.stack([dg0, ds0, dg2, ds2, dg4, ds4, dg6, ds6])
    dmats, dpbias, dhead, dnorms, loss, count = lax.psum(
        (dmats, dpbias, dhead, dnorms, loss, count), ("crop", "row")
    )
    grad_norm = jnp.sqrt(
        jnp.sum(dmats * dmats)
        + jnp.sum(dpbias * dpbias)
        + jnp.sum(dhead * dhead)
        + jnp.sum(dnorms * dnorms)
    )
    factor = jnp.minimum(1.0, CLIP / grad_norm)
    new_mats = adam(mats, dmats * factor, mats_m, mats_v)
    new_pbias = adam(pbias, dpbias * factor, pbias_m, pbias_v)
    new_head = adam(head, dhead * factor, head_m, head_v)
    new_norms = adam(norms, dnorms * factor, norms_m, norms_v)
    return (
        grad_norm,
        loss,
        count,
        new_mats[0],
        new_mats[1],
        new_mats[2],
        new_mats[2].astype(bf),
        new_pbias[0],
        new_pbias[1],
        new_pbias[2],
        new_head[0],
        new_head[1],
        new_head[2],
        new_norms[0],
        new_norms[1],
        new_norms[2],
    )


BF = jnp.bfloat16
FL = jnp.float32
VMEM_LIMIT = 24 * 2**20
SPAN = 2.0**-12
DIGIT = 64


def dot(lhs, rhs, left=1, right=0):
    return lax.dot_general(
        lhs, rhs, (((left,), (right,)), ((), ())), preferred_element_type=FL
    )


def lane_sums(val):
    return jnp.sum(val.T, axis=0, keepdims=True)


def row_norm(val, gain, shift):
    mean = jnp.mean(val, axis=-1, keepdims=True)
    cent = val - mean
    rstd = lax.rsqrt(jnp.mean(cent * cent, axis=-1, keepdims=True) + EPS_NORM)
    unit = cent * rstd
    return (unit * gain + shift).astype(BF), unit, rstd


def row_norm_back(grad, unit, rstd, gain):
    dgain = jnp.sum(grad * unit, axis=0, keepdims=True)
    dshift = jnp.sum(grad, axis=0, keepdims=True)
    dunit = grad * gain
    dval = rstd * (
        dunit
        - jnp.mean(dunit, axis=-1, keepdims=True)
        - unit * jnp.mean(dunit * unit, axis=-1, keepdims=True)
    )
    return dval, dgain, dshift


def iota(shape, dim):
    return lax.broadcasted_iota(jnp.int32, shape, dim)


def fetch(pairs, sems):
    moves = [
        pltpu.make_async_copy(src, dst, sems.at[idx]) for idx, (src, dst) in enumerate(pairs)
    ]
    for move in moves:
        move.start()
    return moves


def start_kernel(
    pair_hbm, norms_hbm, mats_hbm, h0_ref, wl_ref, pair_ref, norms_ref, mats_ref, sems
):
    moves = fetch(
        [(pair_hbm, pair_ref), (norms_hbm, norms_ref), (mats_hbm, mats_ref)], sems
    )
    moves[0].wait()
    moves[1].wait()
    h0_ref[...], _, _ = row_norm(pair_ref[...], norms_ref[0:1], norms_ref[1:2])
    moves[2].wait()
    wl_ref[...] = mats_ref[...].astype(BF)


def block_groups(chips):
    half = chips // 2
    late = [flip for flip in range(chips) if flip % half]
    return (
        [(flip, other) for other in range(2) for flip in (0, half)],
        [(flip, 0) for flip in late],
        [(flip, 1) for flip in late],
    )


def block_at(scal_ref, tag):
    core = scal_ref[3, 0]
    return 2 * (scal_ref[2, 0] ^ tag[0]) + (1 - core if tag[1] else core)


def pair_mask(dims, limit):
    rows, cols, width, _, _ = dims
    spot = iota((rows * cols, width), 0)
    col_ok = spot % cols < limit
    row_in = spot // cols

    def mask_of(block_row):
        return jnp.where(jnp.logical_and(col_ok, row_in + block_row < limit), 1.0, 0.0).astype(FL)

    return mask_of


def own_sides(h0, wl_ref, mask):
    width = h0.shape[1]
    w_own = jnp.concatenate([wl_ref[0], wl_ref[1], wl_ref[4]], axis=1)
    proj = dot(h0, w_own)
    fac = jax.nn.sigmoid(proj[:, width : 2 * width]) * mask
    return fac * proj[:, :width], fac, jax.nn.sigmoid(proj[:, 2 * width :])


def b_block(dims, h0, w_b, col_mask, start, limit):
    rows, cols, width, _, _ = dims
    proj = dot(h0, w_b)
    sig = jax.nn.sigmoid(proj[:, width:])
    lines = []
    for row in range(rows):
        row_ok = jnp.where(start + row < limit, 1.0, 0.0).astype(FL)
        lines.append(sig[row * cols : (row + 1) * cols] * (col_mask * row_ok))
    fac = jnp.concatenate(lines, axis=0)
    return (fac * proj[:, :width]).astype(BF), fac.astype(BF)


def col_mask_of(dims, limit):
    _, cols, width, _, _ = dims
    return jnp.where(iota((cols, width), 0) < limit, 1.0, 0.0).astype(FL)


def x_products(dims, a_rows, side, put):
    rows, cols, width, _, _ = dims
    for row in range(rows):
        b_j = side[row * cols : (row + 1) * cols].astype(FL)
        for idx in range(rows):
            put(idx, row, jnp.sum((a_rows[idx] * b_j).reshape(cols // 8, 8, width), axis=0))


def blocks_kernel(dims, tags, scal_ref, wl_ref, *refs):
    first = tags[0] == (0, 0)
    if not first:
        a_ref, *refs = refs
    h0_refs, refs = refs[: len(tags)], refs[len(tags) :]
    part_ref, side_ref, fac_ref, *refs = refs
    if first:
        a_ref, gate_ref = refs
    rows, cols, width, heads, size = dims
    limit = scal_ref[0, 0]
    if first:
        mask = pair_mask(dims, limit)(scal_ref[1, 0])
        side, _, gate_ref[...] = own_sides(h0_refs[0][...], wl_ref, mask)
        a_ref[...] = side.astype(BF).astype(FL)
    a_rows = [a_ref[idx * cols : (idx + 1) * cols, :] for idx in range(rows)]
    col_mask = col_mask_of(dims, limit)
    w_b = jnp.concatenate([wl_ref[2], wl_ref[3]], axis=1)
    for idx, tag in enumerate(tags):
        start = block_at(scal_ref, tag) * rows
        side, fac = b_block(dims, h0_refs[idx][...], w_b, col_mask, start, limit)
        side_ref[idx] = side
        fac_ref[idx] = fac

        def put(at, row, fold, idx=idx):
            part_ref[at, idx, row * 8 : (row + 1) * 8, :] = fold

        x_products(dims, a_rows, side, put)


def triangle_kernel(
    dims, groups, scal_ref, a_ref, gate_ref, wl_ref, pair_hbm, norms_hbm, pbt_hbm, *refs
):
    tags, before = groups[-1], groups[:-1]
    count = len(before)
    part_refs, side_refs, fac_refs = (refs[at * count : (at + 1) * count] for at in range(3))
    refs = refs[3 * count :]
    h0_refs, refs = refs[: len(tags)], refs[len(tags) :]
    side_hbms, fac_hbms, refs = refs[: count + 1], refs[count + 1 : 2 * count + 2], refs[2 * count + 2 :]
    tb_ref, x_ref, z1_ref, h1_ref, *refs = refs
    pair_ref, norms_ref, pbt_ref, side_ref, fac_ref, part_ref, sems = refs
    rows, cols, width, heads, size = dims
    pairs = rows * cols
    limit = scal_ref[0, 0]
    early_moves = fetch(
        [(norms_hbm, norms_ref), (pair_hbm, pair_ref), (pbt_hbm, pbt_ref)],
        sems.at[pl.ds(0, 3)],
    )
    moves = fetch(
        [*zip(side_refs, side_hbms), *zip(fac_refs, fac_hbms)], sems.at[pl.ds(3, 2 * count)]
    )
    col_mask = col_mask_of(dims, limit)
    w_b = jnp.concatenate([wl_ref[2], wl_ref[3]], axis=1)
    a_rows = [a_ref[idx * cols : (idx + 1) * cols, :] for idx in range(rows)]

    for idx, tag in enumerate(tags):
        block = block_at(scal_ref, tag)
        side, fac = b_block(dims, h0_refs[idx][...], w_b, col_mask, block * rows, limit)
        side_ref[idx] = side
        fac_ref[idx] = fac

        def put(at, row, fold, block=block):
            start = pl.multiple_of((at * cols + block * rows + row) * 8, 8)
            part_ref[pl.ds(start, 8), :] = fold

        x_products(dims, a_rows, side, put)
    moves += fetch(
        [(side_ref, side_hbms[-1]), (fac_ref, fac_hbms[-1])], sems.at[pl.ds(3 + 2 * count, 2)]
    )
    for group, ref in zip(before, part_refs):
        for idx, tag in enumerate(group):
            for at in range(rows):
                start = pl.multiple_of(
                    (at * cols + block_at(scal_ref, tag) * rows) * 8, 8 * rows
                )
                part_ref[pl.ds(start, 8 * rows), :] = ref[at, idx]
    x_val = part_ref[pl.ds(0, pairs, stride=8), :]
    for idx in range(1, 8):
        x_val = x_val + part_ref[pl.ds(idx, pairs, stride=8), :]

    x_ref[...] = x_val
    for move in early_moves:
        move.wait()
    y_low, _, _ = row_norm(x_val, norms_ref[2:3], norms_ref[3:4])
    z1 = pair_ref[...] + gate_ref[...] * dot(y_low, wl_ref[5])
    z1_ref[...] = z1
    h1, _, _ = row_norm(z1, norms_ref[4:5], norms_ref[5:6])
    h1_ref[...] = h1
    tbt = dot(pbt_ref[...].astype(BF), h1, 1, 1).astype(BF).astype(FL)
    half = pairs // 2
    block = jnp.concatenate([tbt[:, :half], tbt[:, half:]], axis=0)
    for idx in range(size):
        tb_ref[idx] = block
    for move in moves:
        move.wait()


def diagonal_block(first, second):
    zero = jnp.zeros(first.shape, first.dtype)
    return jnp.concatenate(
        [
            jnp.concatenate([first, zero], axis=1),
            jnp.concatenate([zero, second], axis=1),
        ],
        axis=0,
    )


def pack_places(dims):
    rows, cols, width, heads, _ = dims
    pairs, lines = rows * cols, heads * cols
    at, places = 0, {}
    for name, tall in (
        ("prob", rows // 2 * lines),
        ("dscore", rows // 2 * lines),
        ("datt", pairs),
        ("u", pairs),
        ("dout2", pairs),
        ("dgate2", pairs),
        ("h2", pairs),
        ("dlog", 2 * cols),
    ):
        places[name] = at
        at += tall
    return places, at


def lane_ramp(width):
    return 1.0 + iota((1, width), 1).astype(FL) / width


def norm_line(small_ref, idx):
    at = small_ref.shape[1] - 8 + idx
    return small_ref[0, at : at + 1, :]


def attention_kernel(
    dims,
    scal_ref,
    tb_ref,
    h1_ref,
    z1_ref,
    wl_ref,
    bins_hbm,
    pb_hbm,
    pb_m_hbm,
    pb_v_hbm,
    head_hbm,
    head_m_hbm,
    head_v_hbm,
    norms_hbm,
    norms_m_hbm,
    norms_v_hbm,
    dtb_ref,
    pack_ref,
    dz2_ref,
    stat_ref,
    kcat_ref,
    qblk_ref,
    pb_ref,
    small_ref,
    vcat_ref,
    bias_ref,
    prob_ref,
    swap_ref,
    bins_ref,
    sems,
):
    rows, cols, width, heads, size = dims
    pairs, lines = rows * cols, heads * cols
    places, _ = pack_places(dims)
    scale = (width // heads) ** (-0.5)
    limit, first_row = scal_ref[0, 0], scal_ref[1, 0]

    def put(name, val):
        pack_ref[places[name] : places[name] + val.shape[0], :] = val

    bins_n = head_hbm.shape[0]
    moves = [(bins_hbm, bins_ref)]
    for idx, (pb, head, norms) in enumerate(
        (
            (pb_hbm, head_hbm, norms_hbm),
            (pb_m_hbm, head_m_hbm, norms_m_hbm),
            (pb_v_hbm, head_v_hbm, norms_v_hbm),
        )
    ):
        moves += [
            (head, small_ref.at[idx, pl.ds(0, bins_n)]),
            (norms, small_ref.at[idx, pl.ds(bins_n, 8)]),
            (pb, pb_ref.at[idx]),
        ]
    moves = fetch(moves, sems)
    w_att = jnp.concatenate([wl_ref[6], wl_ref[7], wl_ref[8], wl_ref[9]], axis=1)
    proj = dot(h1_ref[...], w_att)
    gate2 = jax.nn.sigmoid(proj[:, 3 * width :])
    lane_head = iota((cols, width), 1) // (width // heads)
    zero = jnp.zeros((cols, width), BF)
    for idx in range(rows):
        at, side = idx // 2, idx % 2
        lanes = slice(side * width, (side + 1) * width)
        span = slice(idx * cols, (idx + 1) * cols)
        query = proj[span, :width].astype(BF)
        qblk_ref[at, side * cols : (side + 1) * cols, lanes] = query
        qblk_ref[at, (1 - side) * cols : (2 - side) * cols, lanes] = zero
        for head in range(heads):
            spot = slice(head * cols, (head + 1) * cols)
            keep = lane_head == head
            kcat_ref[at, spot, lanes] = jnp.where(
                keep, proj[span, width : 2 * width], 0.0
            ).astype(BF)
            vcat_ref[at, spot, lanes] = jnp.where(
                keep, proj[span, 2 * width : 3 * width], 0.0
            ).astype(BF)

    for half in range(2):
        for jl in range(2):
            lanes = slice(jl * cols, (jl + 1) * cols)
            got = [
                tb_ref[pl.ds(half * heads + head, size, stride=2 * heads), :][:, lanes]
                for head in range(heads)
            ]
            for duo in range(heads // 2):
                line = jnp.concatenate([got[2 * duo], got[2 * duo + 1]], axis=1)
                bias_ref[duo, pl.ds(2 * half + jl, size, stride=rows), :] = line
                bias_ref[duo, pl.ds(cols + 2 * half + jl, size, stride=rows), :] = line
    bias = jnp.concatenate([bias_ref[duo].T for duo in range(heads // 2)], axis=0)
    key_ok = iota((lines, 2 * cols), 0) % cols < limit
    att = []
    for at in range(rows // 2):
        score = dot(kcat_ref[at], qblk_ref[at], 1, 1) * scale + bias
        score = jnp.where(key_ok, score, -1000000000.0).reshape(heads, cols, 2 * cols)
        top = jnp.max(score, axis=1, keepdims=True)
        grown = jnp.exp(score - top)
        prob = (grown / jnp.sum(grown, axis=1, keepdims=True)).reshape(lines, 2 * cols)
        prob_ref[at] = prob
        low = prob.astype(BF)
        pack_ref[places["prob"] + at * lines : places["prob"] + (at + 1) * lines, :] = low
        both = dot(low, vcat_ref[at], 0, 0)
        att += [both[:cols, :width], both[cols:, width:]]
    att = jnp.concatenate(att, axis=0)
    u_low = (gate2 * att).astype(BF)
    put("u", u_low)
    z2 = z1_ref[...] + dot(u_low, wl_ref[10])
    for move in moves[:3]:
        move.wait()
    h2, unit6, rstd6 = row_norm(z2, norm_line(small_ref, 6), norm_line(small_ref, 7))
    put("h2", h2)
    headt = small_ref[0, :bins_n, :].astype(BF)
    logits = dot(headt, h2, 1, 1)
    spot = iota((1, pairs), 1)
    ok = jnp.logical_and(spot % cols < limit, spot // cols + first_row < limit)
    mask = jnp.where(ok, 1.0, 0.0).astype(FL)
    bins = jnp.concatenate([bins_ref[idx : idx + 1, :] for idx in range(rows)], axis=1)
    onehot = jnp.where(iota(logits.shape, 0) == bins, 1.0, 0.0).astype(FL)
    top = jnp.max(logits, axis=0, keepdims=True)
    lse = top + jnp.log(jnp.sum(jnp.exp(logits - top), axis=0, keepdims=True))
    pick = jnp.sum(logits * onehot, axis=0, keepdims=True)
    loss = jnp.sum(mask * (lse - pick), axis=1, keepdims=True)
    dlog = (mask * (jnp.exp(logits - lse) - onehot)).astype(BF)
    put("dlog", jnp.concatenate([dlog[:, :width], dlog[:, width:]], axis=0))
    dz2, dg6, ds6 = row_norm_back(dot(dlog, headt, 0, 0), unit6, rstd6, norm_line(small_ref, 6))
    dz2_ref[...] = dz2
    stat_ref[0:1, :] = dg6
    stat_ref[1:2, :] = ds6
    used = limit * limit
    ramp = lane_ramp(width)
    stat_ref[2:3, :] = loss * ramp
    stat_ref[3:4, :] = (used // DIGIT).astype(FL) * ramp
    stat_ref[4:5, :] = (used % DIGIT).astype(FL) * ramp
    stat_ref[5:8, :] = jnp.zeros((3, width), FL)
    dout2 = dz2.astype(BF)
    put("dout2", dout2)
    du = dot(dout2, wl_ref[10], 1, 1)
    put("dgate2", (du * att * gate2 * (1.0 - gate2)).astype(BF))
    datt = (du * gate2).astype(BF)
    put("datt", datt)
    total = None
    for at in range(rows // 2):
        first = datt[(2 * at) * cols : (2 * at + 1) * cols]
        second = datt[(2 * at + 1) * cols : (2 * at + 2) * cols]
        block = diagonal_block(first, second)
        dprob = dot(vcat_ref[at], block, 1, 1)
        prob = prob_ref[at]
        inner = jnp.sum((dprob * prob).reshape(heads, cols, 2 * cols), axis=1, keepdims=True)
        dscore = prob.reshape(heads, cols, 2 * cols) * (
            dprob.reshape(heads, cols, 2 * cols) - inner
        )
        low = dscore.reshape(lines, 2 * cols).astype(BF)
        pack_ref[places["dscore"] + at * lines : places["dscore"] + (at + 1) * lines, :] = low
        total = low.astype(FL) if total is None else total + low.astype(FL)
    for duo in range(heads // 2):
        turned = total[duo * 2 * cols : (duo + 1) * 2 * cols].T
        swap_ref[duo] = turned[:cols] + turned[cols:]
    for half in range(2):
        for head in range(heads):
            inside = slice((head % 2) * cols, (head % 2 + 1) * cols)
            line = jnp.concatenate(
                [
                    swap_ref[head // 2, pl.ds(2 * half + jl, size, stride=rows), :][:, inside]
                    for jl in range(2)
                ],
                axis=1,
            )
            dtb_ref[pl.ds(half * heads + head, size, stride=2 * heads), :] = line
    for move in moves[3:]:
        move.wait()


def gradient_kernel(
    dims,
    groups,
    scal_ref,
    dtb_ref,
    pack_ref,
    kcat_ref,
    qblk_ref,
    dz2_ref,
    stat_ref,
    h1_ref,
    x_ref,
    z1_ref,
    small_ref,
    wl_ref,
    pb_ref,
    *refs,
):
    tags = [tag for group in groups for tag in group]
    h0_refs, refs = refs[: len(tags)], refs[len(tags) :]
    count = len(groups)
    side_hbms, fac_hbms, refs = refs[:count], refs[count : 2 * count], refs[2 * count :]
    keep_ref, give_ref, flat_ref, dx_ref, dqkvg_ref, side_ref, fac_ref, sems = refs
    rows, cols, width, heads, size = dims
    pairs = rows * cols
    core = scal_ref[3, 0]
    moves = []
    for arrays, ref in ((side_hbms, side_ref), (fac_hbms, fac_ref)):
        at = 0
        for group, array in zip(groups, arrays):
            moves.append((array, ref.at[pl.ds(at, len(group))]))
            at += len(group)
    moves = fetch(moves, sems)
    lines = heads * cols
    places, _ = pack_places(dims)

    def take(name, tall, skip=0):
        return pack_ref[places[name] + skip : places[name] + skip + tall, :]

    mask = pair_mask(dims, scal_ref[0, 0])(scal_ref[1, 0])
    side, fac, gate = own_sides(h0_refs[0][...], wl_ref, mask)
    a_val = side.astype(BF).astype(FL)
    y_low, unit2, rstd2 = row_norm(x_ref[...], norm_line(small_ref, 2), norm_line(small_ref, 3))
    _, unit4, rstd4 = row_norm(z1_ref[...], norm_line(small_ref, 4), norm_line(small_ref, 5))
    out1 = dot(y_low, wl_ref[5])
    scale = (width // heads) ** (-0.5)
    lane_head = iota((cols, width), 1) // (width // heads)

    def diagonal(val):
        out = jnp.zeros((cols, width), FL)
        for head in range(heads):
            out = jnp.where(lane_head == head, val[head * cols : (head + 1) * cols], out)
        return out

    for at in range(rows // 2):
        dscore = take("dscore", lines, at * lines)
        block = diagonal_block(
            take("datt", cols, 2 * at * cols), take("datt", cols, (2 * at + 1) * cols)
        )
        dquery = dot(dscore, kcat_ref[at], 0, 0)
        dkeys = dot(dscore, qblk_ref[at])
        dvals = dot(take("prob", lines, at * lines), block)
        for side in range(2):
            idx = 2 * at + side
            lanes = slice(side * width, (side + 1) * width)
            span = slice(idx * cols, (idx + 1) * cols)
            dqkvg_ref[span, :width] = (
                dquery[side * cols : (side + 1) * cols, lanes] * scale
            ).astype(BF)
            dqkvg_ref[span, width : 2 * width] = (diagonal(dkeys[:, lanes]) * scale).astype(BF)
            dqkvg_ref[span, 2 * width : 3 * width] = diagonal(dvals[:, lanes]).astype(BF)
    dqkvg_ref[:, 3 * width :] = take("dgate2", pairs)
    dqkvg = dqkvg_ref[...]
    w_att = jnp.concatenate([wl_ref[6], wl_ref[7], wl_ref[8], wl_ref[9]], axis=1)
    dh1 = dot(dqkvg, w_att, 1, 1)
    h1 = h1_ref[...]
    dw_att = dot(h1, dqkvg, 0, 0)
    for idx in range(4):
        flat_ref[(6 + idx) * width : (7 + idx) * width, :] = dw_att[
            :, idx * width : (idx + 1) * width
        ]
    flat_ref[10 * width : 11 * width, :] = dot(take("u", pairs), take("dout2", pairs), 0, 0)
    mats = 11 * width
    dlog = take("dlog", 2 * cols)
    dlog = jnp.concatenate([dlog[:cols], dlog[cols:]], axis=1)
    flat_ref[mats : mats + dlog.shape[0], :] = dot(dlog, take("h2", pairs))
    got = dtb_ref[0]
    for idx in range(1, size):
        got = got + dtb_ref[idx]
    dtbt = jnp.concatenate([got[:heads], got[heads:]], axis=1).astype(BF)
    dpbt = dot(dtbt, h1)
    dh1 = dh1 + dot(dtbt, pb_ref[0].astype(BF), 0, 0)
    dn4, dg4, ds4 = row_norm_back(dh1, unit4, rstd4, norm_line(small_ref, 4))
    dz1 = dz2_ref[...] + dn4
    dout1 = (dz1 * gate).astype(BF)
    dgate = dz1 * out1 * gate * (1.0 - gate)
    dx, dg2, ds2 = row_norm_back(dot(dout1, wl_ref[5], 1, 1), unit2, rstd2, norm_line(small_ref, 2))
    dx_ref[...] = dx.astype(BF).astype(FL)

    for move in moves[:count]:
        move.wait()
    acc = [jnp.zeros((cols, width), FL)] * rows
    for idx, tag in enumerate(tags):
        first = block_at(scal_ref, tag) * rows
        for row in range(rows):
            b_j = side_ref[idx, row * cols : (row + 1) * cols, :].astype(FL)
            acc = [
                acc[at] + dx_ref[pl.ds(at * cols + first + row, 1), :] * b_j
                for at in range(rows)
            ]
    da = jnp.concatenate(acc, axis=0).astype(BF).astype(FL)
    own = jnp.concatenate(
        [
            (da * fac).astype(BF),
            (da * a_val * (1.0 - fac)).astype(BF),
            dgate.astype(BF),
        ],
        axis=1,
    )
    for move in moves[count:]:
        move.wait()
    ones = jnp.ones((16, pairs), BF)

    def products(h0, grads):
        return dot(h0, grads, 0, 0), dot(ones, grads)

    dw_own, sum_own = products(h0_refs[0][...], own)

    a_rows = [a_val[idx * cols : (idx + 1) * cols] for idx in range(rows)]

    dw_b, sum_b = jnp.zeros((width, 2 * width), FL), jnp.zeros((16, 2 * width), FL)
    for idx, tag in enumerate(tags):
        first = block_at(scal_ref, tag) * rows
        lines = []
        for row in range(rows):
            db = dx_ref[pl.ds(first + row, 1), :] * a_rows[0]
            for at in range(1, rows):
                db = db + dx_ref[pl.ds(at * cols + first + row, 1), :] * a_rows[at]
            lines.append(db.astype(BF))
        db = jnp.concatenate(lines, axis=0)
        fac_b = fac_ref[idx]
        grads = jnp.concatenate([db * fac_b, db * (side_ref[idx] * (1.0 - fac_b))], axis=1)
        main, sums = products(h0_refs[idx][...], grads)
        dw_b, sum_b = dw_b + main, sum_b + sums

    parts = [
        (val[:, at * width : (at + 1) * width], sums[:1, at * width : (at + 1) * width])
        for val, sums, at in (
            (dw_own, sum_own, 0),
            (dw_own, sum_own, 1),
            (dw_b, sum_b, 0),
            (dw_b, sum_b, 1),
            (dw_own, sum_own, 2),
        )
    ]
    mixed = jnp.zeros((width, width), FL)
    summed = jnp.zeros((width, width), FL)
    for idx, (part, sums) in enumerate(parts):
        weight = wl_ref[idx].astype(FL)
        flat_ref[idx * width : (idx + 1) * width, :] = part
        mixed = mixed + weight * part
        summed = summed + weight * sums
    ds0 = lane_sums(summed)
    dg0 = (lane_sums(mixed) - norm_line(small_ref, 1) * ds0) / norm_line(small_ref, 0)
    flat_ref[5 * width : 6 * width, :] = dot(y_low, dout1, 0, 0)
    base = mats + dlog.shape[0]
    flat_ref[base : base + heads, :] = dpbt
    flat_ref[base + heads : base + 8, :] = jnp.zeros((8 - heads, width), FL)
    base += 8
    for idx, line in enumerate((dg0, ds0, dg2, ds2, dg4, ds4)):
        flat_ref[base + idx : base + idx + 1, :] = line
    flat_ref[base + 6 : base + 11, :] = stat_ref[0:5, :]
    total = flat_ref.shape[0]
    flat_ref[base + 11 :, :] = jnp.zeros((total - base - 11, width), FL)
    half = total // 2
    keep_ref[...] = flat_ref[pl.ds(pl.multiple_of(core * half, half), half), :]
    give_ref[...] = flat_ref[pl.ds(pl.multiple_of((1 - core) * half, half), half), :]


def update_kernel(
    dims,
    scal_ref,
    mine_ref,
    other_ref,
    mats_ref,
    mats_m_ref,
    mats_v_ref,
    pb_ref,
    small_ref,
    norm_out,
    loss_out,
    count_out,
    mats_m_out,
    mats_v_out,
    mats_out,
    mats_low_out,
    pb_m_out,
    pb_v_out,
    pb_out,
    head_m_out,
    head_v_out,
    head_out,
    norms_m_out,
    norms_v_out,
    norms_out,
    flat_ref,
    scalar_buf,
    small_buf,
    pb_buf,
    m_buf,
    v_buf,
    w_buf,
    low_buf,
    sems,
    small_sems,
):
    rows, cols, width, heads, size = dims
    bins_n = small_ref.shape[1] - 8
    core = scal_ref[3, 0]
    half = mine_ref.shape[0]
    flat_ref[pl.ds(pl.multiple_of(core * half, half), half), :] = mine_ref[...]
    flat_ref[pl.ds(pl.multiple_of((1 - core) * half, half), half), :] = other_ref[...]
    count = mats_ref.shape[0]
    mats = count * width
    base = mats + bins_n
    grads = flat_ref[: base + 16, :]
    square = jnp.sum(grads * grads, axis=0, keepdims=True)
    norm = jnp.sqrt(jnp.sum(square, axis=1, keepdims=True))
    factor = jnp.minimum(1.0, CLIP / norm)
    scalar_buf[0] = norm
    stats = jnp.mean(
        flat_ref[base + 16 : base + 24, :] / lane_ramp(width), axis=1, keepdims=True
    )
    scalar_buf[1] = stats[0:1]
    scalar_buf[2] = (DIGIT * jnp.round(stats[1:2]) + jnp.round(stats[2:3])) / size

    moves = []

    def send(at, idx, buf, out):
        move = pltpu.make_async_copy(buf.at[idx], out.at[idx], sems.at[at, idx])
        move.start()
        moves.append(move)

    def step(weight, grad, first, second):
        return adam(weight, grad * factor, first, second)

    def update_small():
        triples = []
        for at, tall, buf, ref, skip, outs in (
            (mats, bins_n, small_buf, small_ref, 0, (head_m_out, head_v_out, head_out)),
            (base + 8, 8, small_buf, small_ref, bins_n, (norms_m_out, norms_v_out, norms_out)),
            (base, heads, pb_buf, pb_ref, 0, (pb_m_out, pb_v_out, pb_out)),
        ):
            weight, first, second = (ref[idx, skip : skip + tall, :] for idx in range(3))
            now = step(weight, flat_ref[at : at + tall, :], first, second)
            for idx, (val, out) in enumerate(zip(now, outs)):
                buf[idx, skip : skip + tall, :] = val
                triples.append((buf.at[idx, pl.ds(skip, tall)], out))
        triples += [
            (scalar_buf.at[idx], out) for idx, out in enumerate((norm_out, loss_out, count_out))
        ]
        moves.extend(fetch(triples, small_sems))

    for idx in range(count):
        if idx == count // 2:
            update_small()
        m_buf[idx], v_buf[idx], weight = step(
            mats_ref[idx],
            flat_ref[idx * width : (idx + 1) * width, :],
            mats_m_ref[idx],
            mats_v_ref[idx],
        )
        w_buf[idx] = weight
        low_buf[idx] = weight.astype(BF)
        send(0, idx, m_buf, mats_m_out)
        send(1, idx, v_buf, mats_v_out)
        send(2, idx, w_buf, mats_out)
        send(3, idx, low_buf, mats_low_out)
    for move in moves:
        move.wait()


def call(kernel, args, outs, scratch=(), limit=VMEM_LIMIT, flops=10**7):
    spots = {"v": pltpu.VMEM, "h": pltpu.HBM}
    return pl.pallas_call(
        kernel,
        out_shape=[
            pltpu.HBM(shape, kind) if spot == "h" else jax.ShapeDtypeStruct(shape, kind)
            for shape, kind, spot in outs
        ],
        in_specs=[pl.BlockSpec(memory_space=spots[spot]) for _, spot in args],
        out_specs=[pl.BlockSpec(memory_space=spots[spot]) for _, _, spot in outs],
        scratch_shapes=list(scratch),
        compiler_params=pltpu.CompilerParams(vmem_limit_bytes=limit),
        cost_estimate=pl.CostEstimate(flops=flops, bytes_accessed=10**6, transcendentals=0),
    )(
        *(
            pltpu.with_memory_space_constraint(value, pltpu.HBM) if spot == "h" else value
            for value, spot in args
        )
    )


def shrink(val):
    root = jnp.sqrt(jnp.abs(val) * SPAN)
    return jnp.where(val < 0.0, -root, root).astype(jnp.float16)


def grow(root):
    root = root.astype(FL)
    return root * jnp.abs(root) * (1.0 / SPAN)


def same_core_groups(crops, size):
    return [
        [crop * size + idx for crop in range(crops) for idx in range(core, size, 2)]
        for core in range(2)
    ]


def exchange(value, size, flip):
    return lax.ppermute(value, "row", [(idx, idx ^ flip) for idx in range(size)])


def core_swap(value, size):
    return exchange(value, size, 1)


def fast_step(
    crops,
    size,
    pair,
    bins,
    lengths,
    mats,
    mats_m,
    mats_v,
    pbias,
    pbias_m,
    pbias_v,
    head,
    head_m,
    head_v,
    norms,
    norms_m,
    norms_v,
):
    rows, cols, width = pair.shape[1:]
    heads, bins_n = pbias.shape[1], head.shape[1]
    pairs, lines = rows * cols, heads * cols
    dims = (rows, cols, width, heads, size)
    chips = size // 2
    place = lax.axis_index("row")
    scal = jnp.stack([lengths[0], place * rows, place >> 1, place & 1]).astype(jnp.int32)
    scal = jnp.broadcast_to(jnp.pad(scal, (0, 4))[:, None], (8, width))
    start = pair.reshape(pairs, width)
    pbt, headt = pbias.T, head.T

    h0, wl = call(
        start_kernel,
        [(start, "h"), (norms, "h"), (mats, "h")],
        [((pairs, width), BF, "v"), (mats.shape, BF, "v")],
        [
            pltpu.VMEM((pairs, width), FL),
            pltpu.VMEM(norms.shape, FL),
            pltpu.VMEM(mats.shape, FL),
            pltpu.SemaphoreType.DMA((3,)),
        ],
    )
    blocks = {(0, 0): h0}
    half = chips // 2
    blocks[half, 0] = exchange(h0, size, 2 * half)
    for flip in range(1, half):
        blocks[flip, 0] = exchange(h0, size, 2 * flip)
    for flip in range(1, half):
        blocks[half + flip, 0] = exchange(blocks[half, 0], size, 2 * flip)
    for flip in (0, half):
        blocks[flip, 1] = core_swap(blocks[flip, 0], size)
    groups = block_groups(chips)
    parts, sides, facs = [], [], []
    for at, tags in enumerate(groups[:-1]):
        shape = (len(tags), pairs, width)
        res = call(
            functools.partial(blocks_kernel, dims, tags),
            [(scal, "v"), (wl, "v")]
            + [(a_val, "v") for _ in range(at)]
            + [(blocks[tag], "v") for tag in tags],
            [((rows, len(tags), rows * 8, width), FL, "v"), (shape, BF, "v"), (shape, BF, "v")]
            + [((pairs, width), FL, "v")] * (2 - 2 * at),
            flops=10**8 * len(tags),
        )
        parts.append(res[0])
        sides.append(res[1])
        facs.append(res[2])
        if at == 0:
            a_val, gate = res[3:]
            for tag in groups[1]:
                blocks[tag[0], 1] = core_swap(blocks[tag], size)
    shape = (len(groups[-1]), pairs, width)
    count = len(groups)
    *far_sides, tb, x_val, z1, h1 = call(
        functools.partial(triangle_kernel, dims, groups),
        [
            (scal, "v"),
            (a_val, "v"),
            (gate, "v"),
            (wl, "v"),
            (start, "h"),
            (norms, "h"),
            (pbt, "h"),
        ]
        + [(value, "v") for value in parts + sides + facs]
        + [(blocks[tag], "v") for tag in groups[-1]],
        [((len(tags), pairs, width), BF, "h") for tags in groups] * 2
        + [
            ((size, 2 * heads, 2 * cols), FL, "v"),
            ((pairs, width), FL, "v"),
            ((pairs, width), FL, "v"),
            ((pairs, width), BF, "v"),
        ],
        [
            pltpu.VMEM((pairs, width), FL),
            pltpu.VMEM(norms.shape, FL),
            pltpu.VMEM(pbt.shape, FL),
            pltpu.VMEM(shape, BF),
            pltpu.VMEM(shape, BF),
            pltpu.VMEM((pairs * 8, width), FL),
            pltpu.SemaphoreType.DMA((3 + 2 * count,)),
        ],
    )

    tb_all = lax.all_to_all(tb, "row", 0, 0, tiled=True)
    bias_shape = (size * 2 * heads, 2 * cols)
    small_args = (
        pbt,
        pbias_m.T,
        pbias_v.T,
        headt,
        head_m.T,
        head_v.T,
        norms,
        norms_m,
        norms_v,
    )
    dtb, pack, dz2, stat, kcat, qblk, pb_all, small_all = call(
        functools.partial(attention_kernel, dims),
        [
            (scal, "v"),
            (tb_all.reshape(bias_shape), "v"),
            (h1, "v"),
            (z1, "v"),
            (wl, "v"),
            (bins[0], "h"),
        ]
        + [(value, "h") for value in small_args],
        [
            (bias_shape, FL, "v"),
            ((pack_places(dims)[1], width), BF, "v"),
            ((pairs, width), FL, "v"),
            ((8, width), FL, "v"),
            ((rows // 2, lines, 2 * width), BF, "v"),
            ((rows // 2, 2 * cols, 2 * width), BF, "v"),
            ((3, heads, width), FL, "v"),
            ((3, bins_n + norms.shape[0], width), FL, "v"),
        ],
        [
            pltpu.VMEM((rows // 2, lines, 2 * width), BF),
            pltpu.VMEM((heads // 2, 2 * cols, 2 * cols), FL),
            pltpu.VMEM((rows // 2, lines, 2 * cols), FL),
            pltpu.VMEM((heads // 2, cols, 2 * cols), FL),
            pltpu.VMEM((rows, cols), jnp.int32),
            pltpu.SemaphoreType.DMA((10,)),
        ],
    )

    dtb_all = lax.all_to_all(dtb.reshape(size, 2 * heads, 2 * cols), "row", 0, 0, tiled=True)
    used = mats.shape[0] * width + bins_n + 24
    unit = 8 * crops * size
    total = -(-used // unit) * unit
    keep, give = call(
        functools.partial(gradient_kernel, dims, groups),
        [(scal, "v")]
        + [
            (value, "v")
            for value in (dtb_all, pack, kcat, qblk, dz2, stat, h1, x_val, z1, small_all, wl, pb_all)
        ]
        + [(blocks[tag], "v") for tags in groups for tag in tags]
        + [(value, "h") for value in far_sides],
        [((total // 2, width), FL, "v"), ((total // 2, width), FL, "v")],
        [
            pltpu.VMEM((total, width), FL),
            pltpu.VMEM((pairs, width), FL),
            pltpu.VMEM((pairs, 4 * width), BF),
        ]
        + [pltpu.VMEM((size, pairs, width), BF)] * 2
        + [pltpu.SemaphoreType.DMA((2 * len(groups),))],
    )

    half = keep + core_swap(give, size)
    count = crops * chips
    cores = same_core_groups(crops, size)
    axes = ("crop", "row")
    parts = lax.all_to_all(
        shrink(half).reshape(count, -1, width), axes, 0, 0, axis_index_groups=cores, tiled=True
    )
    share = shrink(jnp.sum(grow(parts), axis=0))
    spread = jnp.broadcast_to(share[None], (count,) + share.shape)
    mine = lax.all_to_all(spread, axes, 0, 0, axis_index_groups=cores, tiled=True)
    mine = mine.reshape(total // 2, width)
    other_half = grow(core_swap(mine, size))
    mine = grow(mine)

    number = mats.shape[0]
    big, low = ((number, width, width), FL, "h"), ((number, width, width), BF, "h")
    pb_out, head_out = ((heads, width), FL, "h"), ((bins_n, width), FL, "h")
    norm_out = ((norms.shape[0], width), FL, "h")
    res = call(
        functools.partial(update_kernel, dims),
        [(scal, "v")]
        + [
            (value, "v")
            for value in (mine, other_half, mats, mats_m, mats_v, pb_all, small_all)
        ],
        [((1, 1), FL, "h")] * 3
        + [big, big, big, low]
        + [pb_out] * 3
        + [head_out] * 3
        + [norm_out] * 3,
        [
            pltpu.VMEM((total, width), FL),
            pltpu.VMEM((3, 1, 1), FL),
            pltpu.VMEM((3, bins_n + norms.shape[0], width), FL),
            pltpu.VMEM((3, heads, width), FL),
        ]
        + [pltpu.VMEM((number, width, width), FL)] * 3
        + [
            pltpu.VMEM((number, width, width), BF),
            pltpu.SemaphoreType.DMA((4, number)),
            pltpu.SemaphoreType.DMA((12,)),
        ],
    )
    return (
        *(value.reshape(()) for value in res[:3]),
        *res[3:7],
        *(value.T for value in res[7:13]),
        *res[13:16],
    )


def small_enough(pair, heads, size):
    _, rows, cols, width = pair.shape
    held = 4 * size * rows * cols * width * 4 + 4 * rows * heads * cols * cols * 4
    return (
        held <= 2**24
        and width == 2 * cols
        and rows == 4
        and heads == 4
        and size >= 4
        and size & (size - 1) == 0
        and rows * size == cols
    )


def solution(mesh):
    crops, size = mesh.shape["crop"], mesh.shape["row"]

    def on_device(*args):
        if small_enough(args[0], args[6].shape[1], size):
            return fast_step(crops, size, *args)
        return general_step(*args)

    in_specs = (
        P("crop", "row", None, None),
        P("crop", "row", None),
        P("crop"),
        P(),
        P(),
        P(),
        P(),
        P(),
        P(),
        P(),
        P(),
        P(),
        P(),
        P(),
        P(),
    )
    out_specs = (P(), P(), P(), P(), P(), P(), P(), P(), P(), P(), P(), P(), P(), P(), P(), P())
    return jax.shard_map(
        on_device, mesh=mesh, in_specs=in_specs, out_specs=out_specs, check_vma=False
    )
```

profile of v0, /device:TPU:0, one launch (start us, length us, event | category | flops | bytes accessed | tf_op | source)
XLA Modules:
  0.0 77.8 jit_solution(7865042793487233823)
XLA Ops:
  0.6 1.3 %shard_map.270 = (bf16[256,128]{1,0:T(8,128)(2,1)S(1)}, bf16[11,128,128]{2,1,0:T(8,128)(2,1)S(1)}) custom-call(f32[256,128]{1,0:T(8,128)} %bitcast.29, f32[8,128]{1,0:T(8,128)} %norms_hbm.5, f32[11,128,128]{2,1,0:T(8,128)} %mats_ref.1), custom_call_target="tpu_custom_call" | custom-call | flops 10000000 | bytes 1000000 | tf_op jit(solution)/shard_map/pallas_call | solution.py:953
  1.9 4.1 %collective-permute-start = (bf16[256,128]{1,0:T(8,128)(2,1)S(1)}, bf16[256,128]{1,0:T(8,128)(2,1)S(1)}, u32[]{:S(2)}, u32[]{:S(2)}) collective-permute-start(bf16[256,128]{1,0:T(8,128)(2,1)S(1)} %get-tuple-element.63.refs_0_), channel_id=1, source_target_pairs={{0,8},{1,9},{2,10},{3,11},{4,12},{5,13},{6,14},{7,15},{8,0},{9,1},... | collective-permute-start | bytes 196616 | tf_op jit(solution)/shard_map/ppermute | solution.py:990
  6.0 2.5 %collective-permute-start.5 = (bf16[256,128]{1,0:T(8,128)(2,1)S(1)}, bf16[256,128]{1,0:T(8,128)(2,1)S(1)}, u32[]{:S(2)}, u32[]{:S(2)}) collective-permute-start(bf16[256,128]{1,0:T(8,128)(2,1)S(1)} %get-tuple-element.63.refs_0_), channel_id=1, source_target_pairs={{0,6},{1,7},{2,4},{3,5},{4,2},{5,3},{6,0},{7,1},{8,14},{9,15},{10,... | collective-permute-start | bytes 196616 | tf_op jit(solution)/shard_map/ppermute | solution.py:990
  9.0 0.5 collective-permute-start.3
  10.2 2.6 %collective-permute-start.8 = (bf16[256,128]{1,0:T(8,128)(2,1)S(1)}, bf16[256,128]{1,0:T(8,128)(2,1)S(1)}, u32[]{:S(2)}, u32[]{:S(2)}) collective-permute-start(bf16[256,128]{1,0:T(8,128)(2,1)S(1)} %collective-permute-done.refs_1_), channel_id=1, source_target_pairs={{0,6},{1,7},{2,4},{3,5},{4,2},{5,3},{6,0},{7,1},{8,14},{9,15},{10,... | collective-permute-start | bytes 196616 | tf_op jit(solution)/shard_map/ppermute | solution.py:990
  12.8 0.7 collective-permute-start.7
  13.4 0.8 %collective-permute-start.6 = (bf16[256,128]{1,0:T(8,128)(2,1)S(1)}, bf16[256,128]{1,0:T(8,128)(2,1)S(1)}, u32[]{:S(2)}, u32[]{:S(2)}) collective-permute-start(bf16[256,128]{1,0:T(8,128)(2,1)S(1)} %collective-permute-done.refs_1_), channel_id=1, source_target_pairs={{0,2},{1,3},{2,0},{3,1},{4,6},{5,7},{6,4},{7,5},{8,10},{9,11},{10,... | collective-permute-start | bytes 196616 | tf_op jit(solution)/shard_map/ppermute | solution.py:990
  14.3 0.5 collective-permute-start.11
  14.9 0.8 %collective-permute-done.11.refs_8_.refs_12_ = bf16[256,128]{1,0:T(8,128)(2,1)S(1)} collective-permute-done((bf16[256,128]{1,0:T(8,128)(2,1)S(1)}, bf16[256,128]{1,0:T(8,128)(2,1)S(1)}, u32[]{:S(2)}, u32[]{:S(2)}) %collective-permute-start.11) | collective-permute-done | bytes 65568 | tf_op jit(solution)/shard_map/ppermute | solution.py:990
  16.2 0.9 %collective-permute-done.7.refs_5_.refs_8_ = bf16[256,128]{1,0:T(8,128)(2,1)S(1)} collective-permute-done((bf16[256,128]{1,0:T(8,128)(2,1)S(1)}, bf16[256,128]{1,0:T(8,128)(2,1)S(1)}, u32[]{:S(2)}, u32[]{:S(2)}) %collective-permute-start.7) | collective-permute-done | bytes 65568 | tf_op jit(solution)/shard_map/ppermute | solution.py:990
  17.1 0.6 collective-permute-done.6.refs_4_.refs_7_
  17.7 0.5 collective-permute-start.12
  18.3 0.5 shard_map.271
  18.8 0.6 shard_map.272
  19.4 2.4 %shard_map.273 = (bf16[4,256,128]{2,1,0:T(8,128)(2,1)}, bf16[6,256,128]{2,1,0:T(8,128)(2,1)}, bf16[6,256,128]{2,1,0:T(8,128)(2,1)}, bf16[4,256,128]{2,1,0:T(8,12...) custom-call(s32[8,128]{1,0:T(8,128)S(1)} %broadcast_in_dim.4.scal_re, ...), custom_call_target="tpu_custom_call" | custom-call | flops 10000000 | bytes 1000000 | tf_op jit(solution)/shard_map/pallas_call | solution.py:953
  21.8 10.7 %all_to_all.20 = f32[16,8,128]{2,1,0:T(8,128)S(1)} all-to-all(f32[16,8,128]{2,1,0:T(8,128)S(1)} %get-tuple-element.72), channel_id=1, replica_groups=mesh['crop'=2,'row'=16] {'row'}, dimensions={0} | all-to-all | bytes 131072 | tf_op jit(solution)/shard_map/all_to_all | solution.py:1100
  32.6 2.7 %shard_map.274 = (f32[128,128]{1,0:T(8,128)S(1)}, bf16[2432,128]{1,0:T(8,128)(2,1)S(1)}, f32[256,128]{1,0:T(8,128)S(1)}, f32[8,128]{1,0:T(8,128)S(1)}, bf16[2,25...) custom-call(s32[8,128]{1,0:T(8,128)S(1)} %broadcast_in_dim.4.scal_re, ...), custom_call_target="tpu_custom_call" | custom-call | flops 10000000 | bytes 1000000 | tf_op jit(solution)/shard_map/pallas_call | solution.py:953
  35.2 9.5 %all_to_all.21.dtb_ref = f32[16,8,128]{2,1,0:T(8,128)S(1)} all-to-all(f32[16,8,128]{2,1,0:T(8,128)S(1)} %bitcast.26), channel_id=1, replica_groups=mesh['crop'=2,'row'=16] {'row'}, dimensions={0} | all-to-all | bytes 131072 | tf_op jit(solution)/shard_map/all_to_all | solution.py:1144
  44.7 3.8 %shard_map.275 = (f32[768,128]{1,0:T(8,128)S(1)}, f32[768,128]{1,0:T(8,128)S(1)}) custom-call(s32[8,128]{1,0:T(8,128)S(1)} %broadcast_in_dim.4.scal_ref, f32[16,8,128]{2,1,0:T(8,128)S(1)} %all_to_all.21.dtb_ref, bf16[2432,128]{1,0:T(8,128)(2,1)S(1)} %get-tuple-element.76.pack_ref, bf16[2,256,256]{2,1,0:T(8,128)(2,1)S(1)} %get-tuple-element.77.kcat_ref, ...), custom_call_target="tpu_custom_call" | custom-call | flops 10000000 | bytes 1000000 | tf_op jit(solution)/shard_map/pallas_call | solution.py:953
  48.6 1.7 %collective-permute-done.15 = f32[768,128]{1,0:T(8,128)S(1)} collective-permute-done((f32[768,128]{1,0:T(8,128)S(1)}, f32[768,128]{1,0:T(8,128)S(1)}, u32[]{:S(2)}, u32[]{:S(2)}) %collective-permute-start.15) | collective-permute-done | bytes 393248 | tf_op jit(solution)/shard_map/ppermute | solution.py:990
  50.5 11.7 %all_to_all.22 = f16[16,48,128]{2,1,0:T(8,128)(2,1)S(1)} all-to-all(f16[16,48,128]{2,1,0:T(8,128)(2,1)S(1)} %bitcast.28), channel_id=1, replica_groups={{0,2,4,6,8,10,12,14,16,18,20,22,24,26,28,30},{1,3,5,7,9,11,13,15,17,19,..., dimensions={0} | all-to-all | bytes 393216 | tf_op jit(solution)/shard_map/all_to_all | solution.py:1171
  62.4 11.5 %all_to_all.23 = f16[16,48,128]{2,1,0:T(8,128)(2,1)S(1)} all-to-all(f16[16,48,128]{2,1,0:T(8,128)(2,1)S(1)} %broadcast_in_dim.5), channel_id=1, replica_groups={{0,2,4,6,8,10,12,14,16,18,20,22,24,26,28,30},{1,3,5,7,9,11,13,15,17,19,..., dimensions={0} | all-to-all | bytes 393216 | tf_op jit(solution)/shard_map/all_to_all | solution.py:1176
  73.9 1.4 %collective-permute-done.16 = f16[768,128]{1,0:T(8,128)(2,1)S(1)} collective-permute-done((f16[768,128]{1,0:T(8,128)(2,1)S(1)}, f16[768,128]{1,0:T(8,128)(2,1)S(1)}, u32[]{:S(2)}, u32[]{:S(2)}) %collective-permute-start.16) | collective-permute-done | bytes 196640 | tf_op jit(solution)/shard_map/ppermute | solution.py:990
  75.4 2.4 %shard_map.276 = (f32[1,1]{1,0:T(1,128)}, f32[1,1]{1,0:T(1,128)}, f32[1,1]{1,0:T(1,128)}, f32[11,128,128]{2,1,0:T(8,128)}, f32[11,128,128]{2,1,0:T(8,128)}, /*in...) custom-call(s32[8,128]{1,0:T(8,128)S(1)} %broadcast_in_dim.4.scal_re, ...), custom_call_target="tpu_custom_call" | custom-call | flops 10000000 | bytes 1000000 | tf_op jit(solution)/shard_map/pallas_call | solution.py:953
  (36 shorter events, 1.7 us)
Async XLA Ops:
  1.9 8.2 %collective-permute-start = (bf16[256,128]{1,0:T(8,128)(2,1)S(1)}, bf16[256,128]{1,0:T(8,128)(2,1)S(1)}, u32[]{:S(2)}, u32[]{:S(2)}) collective-permute-start(bf16[256,128]{1,0:T(8,128)(2,1)S(1)} %get-tuple-element.63.refs_0_), channel_id=1, source_target_pairs={{0,8},{1,9},{2,10},{3,11},{4,12},{5,13},{6,14},{7,15},{8,0},{9,1},... | collective-permute-start | bytes 196616 | tf_op jit(solution)/shard_map/ppermute | solution.py:990
  6.0 6.7 %collective-permute-start.5 = (bf16[256,128]{1,0:T(8,128)(2,1)S(1)}, bf16[256,128]{1,0:T(8,128)(2,1)S(1)}, u32[]{:S(2)}, u32[]{:S(2)}) collective-permute-start(bf16[256,128]{1,0:T(8,128)(2,1)S(1)} %get-tuple-element.63.refs_0_), channel_id=1, source_target_pairs={{0,6},{1,7},{2,4},{3,5},{4,2},{5,3},{6,0},{7,1},{8,14},{9,15},{10,... | collective-permute-start | bytes 196616 | tf_op jit(solution)/shard_map/ppermute | solution.py:990
  8.5 4.9 %collective-permute-start.4 = (bf16[256,128]{1,0:T(8,128)(2,1)S(1)}, bf16[256,128]{1,0:T(8,128)(2,1)S(1)}, u32[]{:S(2)}, u32[]{:S(2)}) collective-permute-start(bf16[256,128]{1,0:T(8,128)(2,1)S(1)} %get-tuple-element.63.refs_0_), channel_id=1, source_target_pairs={{0,4},{1,5},{2,6},{3,7},{4,0},{5,1},{6,2},{7,3},{8,12},{9,13},{10,... | collective-permute-start | bytes 196616 | tf_op jit(solution)/shard_map/ppermute | solution.py:990
  9.0 5.3 %collective-permute-start.3 = (bf16[256,128]{1,0:T(8,128)(2,1)S(1)}, bf16[256,128]{1,0:T(8,128)(2,1)S(1)}, u32[]{:S(2)}, u32[]{:S(2)}) collective-permute-start(bf16[256,128]{1,0:T(8,128)(2,1)S(1)} %get-tuple-element.63.refs_0_), channel_id=1, source_target_pairs={{0,2},{1,3},{2,0},{3,1},{4,6},{5,7},{6,4},{7,5},{8,10},{9,11},{10,... | collective-permute-start | bytes 196616 | tf_op jit(solution)/shard_map/ppermute | solution.py:990
  9.5 4.8 %collective-permute-start.1 = (bf16[256,128]{1,0:T(8,128)(2,1)S(1)}, bf16[256,128]{1,0:T(8,128)(2,1)S(1)}, u32[]{:S(2)}, u32[]{:S(2)}) collective-permute-start(bf16[256,128]{1,0:T(8,128)(2,1)S(1)} %get-tuple-element.63.refs_0_), channel_id=1, source_target_pairs={{0,1},{1,0},{2,3},{3,2},{4,5},{5,4},{6,7},{7,6},{8,9},{9,8},{10,11... | collective-permute-start | bytes 196616 | tf_op jit(solution)/shard_map/ppermute | solution.py:990
  10.2 5.9 %collective-permute-start.8 = (bf16[256,128]{1,0:T(8,128)(2,1)S(1)}, bf16[256,128]{1,0:T(8,128)(2,1)S(1)}, u32[]{:S(2)}, u32[]{:S(2)}) collective-permute-start(bf16[256,128]{1,0:T(8,128)(2,1)S(1)} %collective-permute-done.refs_1_), channel_id=1, source_target_pairs={{0,6},{1,7},{2,4},{3,5},{4,2},{5,3},{6,0},{7,1},{8,14},{9,15},{10,... | collective-permute-start | bytes 196616 | tf_op jit(solution)/shard_map/ppermute | solution.py:990
  12.8 4.3 %collective-permute-start.7 = (bf16[256,128]{1,0:T(8,128)(2,1)S(1)}, bf16[256,128]{1,0:T(8,128)(2,1)S(1)}, u32[]{:S(2)}, u32[]{:S(2)}) collective-permute-start(bf16[256,128]{1,0:T(8,128)(2,1)S(1)} %collective-permute-done.refs_1_), channel_id=1, source_target_pairs={{0,4},{1,5},{2,6},{3,7},{4,0},{5,1},{6,2},{7,3},{8,12},{9,13},{10,... | collective-permute-start | bytes 196616 | tf_op jit(solution)/shard_map/ppermute | solution.py:990
  13.4 4.3 %collective-permute-start.6 = (bf16[256,128]{1,0:T(8,128)(2,1)S(1)}, bf16[256,128]{1,0:T(8,128)(2,1)S(1)}, u32[]{:S(2)}, u32[]{:S(2)}) collective-permute-start(bf16[256,128]{1,0:T(8,128)(2,1)S(1)} %collective-permute-done.refs_1_), channel_id=1, source_target_pairs={{0,2},{1,3},{2,0},{3,1},{4,6},{5,7},{6,4},{7,5},{8,10},{9,11},{10,... | collective-permute-start | bytes 196616 | tf_op jit(solution)/shard_map/ppermute | solution.py:990
  14.3 3.4 %collective-permute-start.2 = (bf16[256,128]{1,0:T(8,128)(2,1)S(1)}, bf16[256,128]{1,0:T(8,128)(2,1)S(1)}, u32[]{:S(2)}, u32[]{:S(2)}) collective-permute-start(bf16[256,128]{1,0:T(8,128)(2,1)S(1)} %collective-permute-done.refs_1_), channel_id=1, source_target_pairs={{0,1},{1,0},{2,3},{3,2},{4,5},{5,4},{6,7},{7,6},{8,9},{9,8},{10,11... | collective-permute-start | bytes 196616 | tf_op jit(solution)/shard_map/ppermute | solution.py:990
  14.3 1.4 %collective-permute-start.11 = (bf16[256,128]{1,0:T(8,128)(2,1)S(1)}, bf16[256,128]{1,0:T(8,128)(2,1)S(1)}, u32[]{:S(2)}, u32[]{:S(2)}) collective-permute-start(bf16[256,128]{1,0:T(8,128)(2,1)S(1)} %collective-permute-done.5.refs_3_.refs_6_), channel_id=1, source_target_pairs={{0,1},{1,0},{2,3},{3,2},{4,5},{5,4},{6,7},{7,6},{8,9},{9,8},{10,11... | collective-permute-start | bytes 196616 | tf_op jit(solution)/shard_map/ppermute | solution.py:990
  15.7 3.7 %collective-permute-start.10 = (bf16[256,128]{1,0:T(8,128)(2,1)S(1)}, bf16[256,128]{1,0:T(8,128)(2,1)S(1)}, u32[]{:S(2)}, u32[]{:S(2)}) collective-permute-start(bf16[256,128]{1,0:T(8,128)(2,1)S(1)} %collective-permute-done.4.refs_2_.refs_5_), channel_id=1, source_target_pairs={{0,1},{1,0},{2,3},{3,2},{4,5},{5,4},{6,7},{7,6},{8,9},{9,8},{10,11... | collective-permute-start | bytes 196616 | tf_op jit(solution)/shard_map/ppermute | solution.py:990
  16.0 3.3 %collective-permute-start.9 = (bf16[256,128]{1,0:T(8,128)(2,1)S(1)}, bf16[256,128]{1,0:T(8,128)(2,1)S(1)}, u32[]{:S(2)}, u32[]{:S(2)}) collective-permute-start(bf16[256,128]{1,0:T(8,128)(2,1)S(1)} %collective-permute-done.3.refs_1_.refs_4_), channel_id=1, source_target_pairs={{0,1},{1,0},{2,3},{3,2},{4,5},{5,4},{6,7},{7,6},{8,9},{9,8},{10,11... | collective-permute-start | bytes 196616 | tf_op jit(solution)/shard_map/ppermute | solution.py:990
  17.1 2.3 %collective-permute-start.14 = (bf16[256,128]{1,0:T(8,128)(2,1)S(1)}, bf16[256,128]{1,0:T(8,128)(2,1)S(1)}, u32[]{:S(2)}, u32[]{:S(2)}) collective-permute-start(bf16[256,128]{1,0:T(8,128)(2,1)S(1)} %collective-permute-done.8.refs_6_.refs_9_), channel_id=1, source_target_pairs={{0,1},{1,0},{2,3},{3,2},{4,5},{5,4},{6,7},{7,6},{8,9},{9,8},{10,11... | collective-permute-start | bytes 196616 | tf_op jit(solution)/shard_map/ppermute | solution.py:990
  17.7 1.7 %collective-permute-start.13 = (bf16[256,128]{1,0:T(8,128)(2,1)S(1)}, bf16[256,128]{1,0:T(8,128)(2,1)S(1)}, u32[]{:S(2)}, u32[]{:S(2)}) collective-permute-start(bf16[256,128]{1,0:T(8,128)(2,1)S(1)} %collective-permute-done.7.refs_5_.refs_8_), channel_id=1, source_target_pairs={{0,1},{1,0},{2,3},{3,2},{4,5},{5,4},{6,7},{7,6},{8,9},{9,8},{10,11... | collective-permute-start | bytes 196616 | tf_op jit(solution)/shard_map/ppermute | solution.py:990
  17.7 1.7 %collective-permute-start.12 = (bf16[256,128]{1,0:T(8,128)(2,1)S(1)}, bf16[256,128]{1,0:T(8,128)(2,1)S(1)}, u32[]{:S(2)}, u32[]{:S(2)}) collective-permute-start(bf16[256,128]{1,0:T(8,128)(2,1)S(1)} %collective-permute-done.6.refs_4_.refs_7_), channel_id=1, source_target_pairs={{0,1},{1,0},{2,3},{3,2},{4,5},{5,4},{6,7},{7,6},{8,9},{9,8},{10,11... | collective-permute-start | bytes 196616 | tf_op jit(solution)/shard_map/ppermute | solution.py:990
  48.5 1.8 %collective-permute-start.15 = (f32[768,128]{1,0:T(8,128)S(1)}, f32[768,128]{1,0:T(8,128)S(1)}, u32[]{:S(2)}, u32[]{:S(2)}) collective-permute-start(f32[768,128]{1,0:T(8,128)S(1)} %get-tuple-element.91), channel_id=1, source_target_pairs={{0,1},{1,0},{2,3},{3,2},{4,5},{5,4},{6,7},{7,6},{8,9},{9,8},{10,11... | collective-permute-start | bytes 1179656 | tf_op jit(solution)/shard_map/ppermute | solution.py:990
  50.5 24.8 %copy-start.2 = (f32[11,128,128]{2,1,0:T(8,128)S(1)}, f32[11,128,128]{2,1,0:T(8,128)}, u32[]{:S(2)}) copy-start(f32[11,128,128]{2,1,0:T(8,128)} %mats_v_ref.1) | copy-start | bytes 2162692
  62.3 13.0 %copy-start = (f32[11,128,128]{2,1,0:T(8,128)S(1)}, f32[11,128,128]{2,1,0:T(8,128)}, u32[]{:S(2)}) copy-start(f32[11,128,128]{2,1,0:T(8,128)} %mats_ref.1) | copy-start | bytes 2162692
  62.4 13.0 %copy-start.1 = (f32[11,128,128]{2,1,0:T(8,128)S(1)}, f32[11,128,128]{2,1,0:T(8,128)}, u32[]{:S(2)}) copy-start(f32[11,128,128]{2,1,0:T(8,128)} %mats_m_ref.1) | copy-start | bytes 2162692
  73.9 1.4 %collective-permute-start.16 = (f16[768,128]{1,0:T(8,128)(2,1)S(1)}, f16[768,128]{1,0:T(8,128)(2,1)S(1)}, u32[]{:S(2)}, u32[]{:S(2)}) collective-permute-start(f16[768,128]{1,0:T(8,128)(2,1)S(1)} %bitcast.27), channel_id=1, source_target_pairs={{0,1},{1,0},{2,3},{3,2},{4,5},{5,4},{6,7},{7,6},{8,9},{9,8},{10,11... | collective-permute-start | bytes 589832 | tf_op jit(solution)/shard_map/ppermute | solution.py:990
where the time goes:
time: 78.2 us; the launch traced here: 77.8 us
  blocking collectives  43.4 us (55%)
  Pallas kernels  13.6 us (17%)
  starting transfers between devices  13.3 us (17%)
  waiting for transfers between devices  5.43 us (7%)
  between operations  1.49 us (2%)
    pallas_call x7, Pallas kernels, call(): pl.pallas_call(kernel, out_shape=[pltpu.HBM(shape, kind) if spot == 'h' e...  13.6 us
    ppermute x17, starting transfers between devices, exchange(): lax.ppermute(value, 'row', [(idx, idx ^ flip) for idx in range(size)])  13.3 us
    all_to_all x1, blocking collectives, fast_step(): lax.all_to_all(shrink(half).reshape(count, -1, width), axes, 0, 0, axis_i...  11.7 us
    all_to_all x1, blocking collectives, fast_step(): lax.all_to_all(spread, axes, 0, 0, axis_index_groups=cores, tiled=True)  11.5 us
    all_to_all x1, blocking collectives, fast_step(): tb_all = lax.all_to_all(tb, 'row', 0, 0, tiled=True)  10.7 us
    all_to_all x1, blocking collectives, fast_step(): lax.all_to_all(dtb.reshape(size, 2 * heads, 2 * cols), 'row', 0, 0, tiled...  9.48 us
    ppermute x17, waiting for transfers between devices, exchange(): lax.ppermute(value, 'row', [(idx, idx ^ flip) for idx in range(size)])  5.43 us
  transfers between devices with their start and end apart: 17, of which 5 were waited for; matrix products, arithmetic and copies ran while one was open for 0% of the time, Pallas kernels for 1%

commit v1 on v0

--- a/solution.py
+++ b/solution.py
@@ -303,8 +303,7 @@
     half = chips // 2
     late = [flip for flip in range(chips) if flip % half]
     return (
-        [(flip, other) for other in range(2) for flip in (0, half)],
-        [(flip, 0) for flip in late],
+        [(flip, other) for other in range(2) for flip in (0, half)] + [(flip, 0) for flip in late],
         [(flip, 1) for flip in late],
     )
 
@@ -1042,7 +1041,7 @@
         blocks[flip, 0] = exchange(h0, size, 2 * flip)
     for flip in range(1, half):
         blocks[half + flip, 0] = exchange(blocks[half, 0], size, 2 * flip)
-    for flip in (0, half):
+    for flip in range(chips):
         blocks[flip, 1] = core_swap(blocks[flip, 0], size)
     groups = block_groups(chips)
     parts, sides, facs = [], [], []
@@ -1062,8 +1061,6 @@
         facs.append(res[2])
         if at == 0:
             a_val, gate = res[3:]
-            for tag in groups[1]:
-                blocks[tag[0], 1] = core_swap(blocks[tag], size)
     shape = (len(groups[-1]), pairs, width)
     count = len(groups)
     *far_sides, tb, x_val, z1, h1 = call(
@@ -1164,7 +1161,7 @@
         + [pltpu.SemaphoreType.DMA((2 * len(groups),))],
     )
 
-    half = keep + core_swap(give, size)
+    half = keep + grow(core_swap(shrink(give), size))
     count = crops * chips
     cores = same_core_groups(crops, size)
     axes = ("crop", "row")

time: 78.2 us -> 78 us (level)
    pallas_call x7 -> x6, Pallas kernels: 13.6 us -> 13.5 us  [call(): pl.pallas_call(kernel, out_shape=[pltpu.HBM(shape, kind) if spot == 'h' e...]
where the time goes in v1:
time: 78 us; the launch traced here: 77.6 us
  blocking collectives  43.4 us (56%)
  Pallas kernels  13.5 us (17%)
  starting transfers between devices  13.3 us (17%)
  waiting for transfers between devices  5.15 us (7%)
  between operations  1.49 us (2%)
    pallas_call x6, Pallas kernels, call(): pl.pallas_call(kernel, out_shape=[pltpu.HBM(shape, kind) if spot == 'h' e...  13.5 us
    ppermute x17, starting transfers between devices, exchange(): lax.ppermute(value, 'row', [(idx, idx ^ flip) for idx in range(size)])  13.3 us
    all_to_all x1, blocking collectives, fast_step(): lax.all_to_all(shrink(half).reshape(count, -1, width), axes, 0, 0, axis_i...  11.7 us
    all_to_all x1, blocking collectives, fast_step(): lax.all_to_all(spread, axes, 0, 0, axis_index_groups=cores, tiled=True)  11.5 us
    all_to_all x1, blocking collectives, fast_step(): tb_all = lax.all_to_all(tb, 'row', 0, 0, tiled=True)  10.7 us
    all_to_all x1, blocking collectives, fast_step(): lax.all_to_all(dtb.reshape(size, 2 * heads, 2 * cols), 'row', 0, 0, tiled...  9.48 us
    ppermute x17, waiting for transfers between devices, exchange(): lax.ppermute(value, 'row', [(idx, idx ^ flip) for idx in range(size)])  5.15 us
  transfers between devices with their start and end apart: 17, of which 5 were waited for; matrix products, arithmetic and copies ran while one was open for 0% of the time, Pallas kernels for 1%

profile of v1, /device:TPU:0, one launch (start us, length us, event | category | flops | bytes accessed | tf_op | source)
XLA Modules:
  0.0 77.6 jit_solution(6110929792933932832)
XLA Ops:
  0.6 1.3 %shard_map.270 = (bf16[256,128]{1,0:T(8,128)(2,1)S(1)}, bf16[11,128,128]{2,1,0:T(8,128)(2,1)S(1)}) custom-call(f32[256,128]{1,0:T(8,128)} %bitcast.29, f32[8,128]{1,0:T(8,128)} %norms_hbm.5, f32[11,128,128]{2,1,0:T(8,128)} %mats_ref.1), custom_call_target="tpu_custom_call" | custom-call | flops 10000000 | bytes 1000000 | tf_op jit(solution)/shard_map/pallas_call | solution.py:952
  1.9 4.1 %collective-permute-start = (bf16[256,128]{1,0:T(8,128)(2,1)S(1)}, bf16[256,128]{1,0:T(8,128)(2,1)S(1)}, u32[]{:S(2)}, u32[]{:S(2)}) collective-permute-start(bf16[256,128]{1,0:T(8,128)(2,1)S(1)} %get-tuple-element.58.refs_0_), channel_id=1, source_target_pairs={{0,8},{1,9},{2,10},{3,11},{4,12},{5,13},{6,14},{7,15},{8,0},{9,1},... | collective-permute-start | bytes 196616 | tf_op jit(solution)/shard_map/ppermute | solution.py:989
  6.0 2.5 %collective-permute-start.5 = (bf16[256,128]{1,0:T(8,128)(2,1)S(1)}, bf16[256,128]{1,0:T(8,128)(2,1)S(1)}, u32[]{:S(2)}, u32[]{:S(2)}) collective-permute-start(bf16[256,128]{1,0:T(8,128)(2,1)S(1)} %get-tuple-element.58.refs_0_), channel_id=1, source_target_pairs={{0,6},{1,7},{2,4},{3,5},{4,2},{5,3},{6,0},{7,1},{8,14},{9,15},{10,... | collective-permute-start | bytes 196616 | tf_op jit(solution)/shard_map/ppermute | solution.py:989
  8.5 0.4 collective-permute-start.4
  9.0 0.5 collective-permute-start.3
  10.2 2.6 %collective-permute-start.8 = (bf16[256,128]{1,0:T(8,128)(2,1)S(1)}, bf16[256,128]{1,0:T(8,128)(2,1)S(1)}, u32[]{:S(2)}, u32[]{:S(2)}) collective-permute-start(bf16[256,128]{1,0:T(8,128)(2,1)S(1)} %collective-permute-done.refs_1_), channel_id=1, source_target_pairs={{0,6},{1,7},{2,4},{3,5},{4,2},{5,3},{6,0},{7,1},{8,14},{9,15},{10,... | collective-permute-start | bytes 196616 | tf_op jit(solution)/shard_map/ppermute | solution.py:989
  12.8 0.7 collective-permute-start.7
  13.4 0.8 %collective-permute-start.6 = (bf16[256,128]{1,0:T(8,128)(2,1)S(1)}, bf16[256,128]{1,0:T(8,128)(2,1)S(1)}, u32[]{:S(2)}, u32[]{:S(2)}) collective-permute-start(bf16[256,128]{1,0:T(8,128)(2,1)S(1)} %collective-permute-done.refs_1_), channel_id=1, source_target_pairs={{0,2},{1,3},{2,0},{3,1},{4,6},{5,7},{6,4},{7,5},{8,10},{9,11},{10,... | collective-permute-start | bytes 196616 | tf_op jit(solution)/shard_map/ppermute | solution.py:989
  14.3 0.5 collective-permute-start.11
  14.9 0.8 %collective-permute-done.11.refs_5_.refs_12_ = bf16[256,128]{1,0:T(8,128)(2,1)S(1)} collective-permute-done((bf16[256,128]{1,0:T(8,128)(2,1)S(1)}, bf16[256,128]{1,0:T(8,128)(2,1)S(1)}, u32[]{:S(2)}, u32[]{:S(2)}) %collective-permute-start.11) | collective-permute-done | bytes 65568 | tf_op jit(solution)/shard_map/ppermute | solution.py:989
  16.2 0.9 %collective-permute-done.7.refs_8_ = bf16[256,128]{1,0:T(8,128)(2,1)S(1)} collective-permute-done((bf16[256,128]{1,0:T(8,128)(2,1)S(1)}, bf16[256,128]{1,0:T(8,128)(2,1)S(1)}, u32[]{:S(2)}, u32[]{:S(2)}) %collective-permute-start.7) | collective-permute-done | bytes 65568 | tf_op jit(solution)/shard_map/ppermute | solution.py:989
  17.1 0.6 collective-permute-done.6.refs_7_
  17.7 0.5 collective-permute-start.12
  18.3 0.9 %shard_map.271 = (f32[4,10,32,128]{3,2,1,0:T(8,128)S(1)}, bf16[10,256,128]{2,1,0:T(8,128)(2,1)S(1)}, bf16[10,256,128]{2,1,0:T(8,128)(2,1)S(1)}, f32[256,128]{1,0:T(8,128)S(1)}, f32[256,128]{1,0:T(8,128)S(1)}) custom-call(s32[8,128]{1,0:T(8,128)S(1)} %broadcast_in_dim.4.scal_ref, bf16[11,128,128]{2,1,0:T(8,128)(2,1)S(1)} %get-tuple-element.57.wl_ref, ...), custom_call_target="tpu_custom_call" | custom-call | flops 1000000000 | bytes 1000000 | tf_op jit(solution)/shard_map/pallas_call | solution.py:952
  19.3 2.4 %shard_map.272 = (bf16[10,256,128]{2,1,0:T(8,128)(2,1)}, bf16[6,256,128]{2,1,0:T(8,128)(2,1)}, bf16[10,256,128]{2,1,0:T(8,128)(2,1)}, bf16[6,256,128]{2,1,0:T(8,...) custom-call(s32[8,128]{1,0:T(8,128)S(1)} %broadcast_in_dim.4.scal_re, ...), custom_call_target="tpu_custom_call" | custom-call | flops 10000000 | bytes 1000000 | tf_op jit(solution)/shard_map/pallas_call | solution.py:952
  21.7 10.7 %all_to_all.20 = f32[16,8,128]{2,1,0:T(8,128)S(1)} all-to-all(f32[16,8,128]{2,1,0:T(8,128)S(1)} %get-tuple-element.64), channel_id=1, replica_groups=mesh['crop'=2,'row'=16] {'row'}, dimensions={0} | all-to-all | bytes 131072 | tf_op jit(solution)/shard_map/all_to_all | solution.py:1097
  32.4 2.7 %shard_map.273 = (f32[128,128]{1,0:T(8,128)S(1)}, bf16[2432,128]{1,0:T(8,128)(2,1)S(1)}, f32[256,128]{1,0:T(8,128)S(1)}, f32[8,128]{1,0:T(8,128)S(1)}, bf16[2,25...) custom-call(s32[8,128]{1,0:T(8,128)S(1)} %broadcast_in_dim.4.scal_re, ...), custom_call_target="tpu_custom_call" | custom-call | flops 10000000 | bytes 1000000 | tf_op jit(solution)/shard_map/pallas_call | solution.py:952
  35.1 9.5 %all_to_all.21.dtb_ref = f32[16,8,128]{2,1,0:T(8,128)S(1)} all-to-all(f32[16,8,128]{2,1,0:T(8,128)S(1)} %bitcast.26), channel_id=1, replica_groups=mesh['crop'=2,'row'=16] {'row'}, dimensions={0} | all-to-all | bytes 131072 | tf_op jit(solution)/shard_map/all_to_all | solution.py:1141
  44.6 3.8 %shard_map.274 = (f32[768,128]{1,0:T(8,128)S(1)}, f32[768,128]{1,0:T(8,128)S(1)}) custom-call(s32[8,128]{1,0:T(8,128)S(1)} %broadcast_in_dim.4.scal_ref, f32[16,8,128]{2,1,0:T(8,128)S(1)} %all_to_all.21.dtb_ref, bf16[2432,128]{1,0:T(8,128)(2,1)S(1)} %get-tuple-element.68.pack_ref, bf16[2,256,256]{2,1,0:T(8,128)(2,1)S(1)} %get-tuple-element.69.kcat_ref, ...), custom_call_target="tpu_custom_call" | custom-call | flops 10000000 | bytes 1000000 | tf_op jit(solution)/shard_map/pallas_call | solution.py:952
  48.6 1.4 %collective-permute-done.15 = f16[768,128]{1,0:T(8,128)(2,1)S(1)} collective-permute-done((f16[768,128]{1,0:T(8,128)(2,1)S(1)}, f16[768,128]{1,0:T(8,128)(2,1)S(1)}, u32[]{:S(2)}, u32[]{:S(2)}) %collective-permute-start.15) | collective-permute-done | bytes 196640 | tf_op jit(solution)/shard_map/ppermute | solution.py:989
  50.3 11.7 %all_to_all.22 = f16[16,48,128]{2,1,0:T(8,128)(2,1)S(1)} all-to-all(f16[16,48,128]{2,1,0:T(8,128)(2,1)S(1)} %bitcast.28), channel_id=1, replica_groups={{0,2,4,6,8,10,12,14,16,18,20,22,24,26,28,30},{1,3,5,7,9,11,13,15,17,19,..., dimensions={0} | all-to-all | bytes 393216 | tf_op jit(solution)/shard_map/all_to_all | solution.py:1168
  62.2 11.5 %all_to_all.23 = f16[16,48,128]{2,1,0:T(8,128)(2,1)S(1)} all-to-all(f16[16,48,128]{2,1,0:T(8,128)(2,1)S(1)} %broadcast_in_dim.5), channel_id=1, replica_groups={{0,2,4,6,8,10,12,14,16,18,20,22,24,26,28,30},{1,3,5,7,9,11,13,15,17,19,..., dimensions={0} | all-to-all | bytes 393216 | tf_op jit(solution)/shard_map/all_to_all | solution.py:1173
  73.7 1.4 %collective-permute-done.16 = f16[768,128]{1,0:T(8,128)(2,1)S(1)} collective-permute-done((f16[768,128]{1,0:T(8,128)(2,1)S(1)}, f16[768,128]{1,0:T(8,128)(2,1)S(1)}, u32[]{:S(2)}, u32[]{:S(2)}) %collective-permute-start.16) | collective-permute-done | bytes 196640 | tf_op jit(solution)/shard_map/ppermute | solution.py:989
  75.2 2.4 %shard_map.275 = (f32[1,1]{1,0:T(1,128)}, f32[1,1]{1,0:T(1,128)}, f32[1,1]{1,0:T(1,128)}, f32[11,128,128]{2,1,0:T(8,128)}, f32[11,128,128]{2,1,0:T(8,128)}, /*in...) custom-call(s32[8,128]{1,0:T(8,128)S(1)} %broadcast_in_dim.4.scal_re, ...), custom_call_target="tpu_custom_call" | custom-call | flops 10000000 | bytes 1000000 | tf_op jit(solution)/shard_map/pallas_call | solution.py:952
  (36 shorter events, 1.5 us)
Async XLA Ops:
  1.9 8.2 %collective-permute-start = (bf16[256,128]{1,0:T(8,128)(2,1)S(1)}, bf16[256,128]{1,0:T(8,128)(2,1)S(1)}, u32[]{:S(2)}, u32[]{:S(2)}) collective-permute-start(bf16[256,128]{1,0:T(8,128)(2,1)S(1)} %get-tuple-element.58.refs_0_), channel_id=1, source_target_pairs={{0,8},{1,9},{2,10},{3,11},{4,12},{5,13},{6,14},{7,15},{8,0},{9,1},... | collective-permute-start | bytes 196616 | tf_op jit(solution)/shard_map/ppermute | solution.py:989
  6.0 6.7 %collective-permute-start.5 = (bf16[256,128]{1,0:T(8,128)(2,1)S(1)}, bf16[256,128]{1,0:T(8,128)(2,1)S(1)}, u32[]{:S(2)}, u32[]{:S(2)}) collective-permute-start(bf16[256,128]{1,0:T(8,128)(2,1)S(1)} %get-tuple-element.58.refs_0_), channel_id=1, source_target_pairs={{0,6},{1,7},{2,4},{3,5},{4,2},{5,3},{6,0},{7,1},{8,14},{9,15},{10,... | collective-permute-start | bytes 196616 | tf_op jit(solution)/shard_map/ppermute | solution.py:989
  8.5 4.9 %collective-permute-start.4 = (bf16[256,128]{1,0:T(8,128)(2,1)S(1)}, bf16[256,128]{1,0:T(8,128)(2,1)S(1)}, u32[]{:S(2)}, u32[]{:S(2)}) collective-permute-start(bf16[256,128]{1,0:T(8,128)(2,1)S(1)} %get-tuple-element.58.refs_0_), channel_id=1, source_target_pairs={{0,4},{1,5},{2,6},{3,7},{4,0},{5,1},{6,2},{7,3},{8,12},{9,13},{10,... | collective-permute-start | bytes 196616 | tf_op jit(solution)/shard_map/ppermute | solution.py:989
  9.0 5.3 %collective-permute-start.3 = (bf16[256,128]{1,0:T(8,128)(2,1)S(1)}, bf16[256,128]{1,0:T(8,128)(2,1)S(1)}, u32[]{:S(2)}, u32[]{:S(2)}) collective-permute-start(bf16[256,128]{1,0:T(8,128)(2,1)S(1)} %get-tuple-element.58.refs_0_), channel_id=1, source_target_pairs={{0,2},{1,3},{2,0},{3,1},{4,6},{5,7},{6,4},{7,5},{8,10},{9,11},{10,... | collective-permute-start | bytes 196616 | tf_op jit(solution)/shard_map/ppermute | solution.py:989
  9.5 4.8 %collective-permute-start.1 = (bf16[256,128]{1,0:T(8,128)(2,1)S(1)}, bf16[256,128]{1,0:T(8,128)(2,1)S(1)}, u32[]{:S(2)}, u32[]{:S(2)}) collective-permute-start(bf16[256,128]{1,0:T(8,128)(2,1)S(1)} %get-tuple-element.58.refs_0_), channel_id=1, source_target_pairs={{0,1},{1,0},{2,3},{3,2},{4,5},{5,4},{6,7},{7,6},{8,9},{9,8},{10,11... | collective-permute-start | bytes 196616 | tf_op jit(solution)/shard_map/ppermute | solution.py:989
  10.2 5.9 %collective-permute-start.8 = (bf16[256,128]{1,0:T(8,128)(2,1)S(1)}, bf16[256,128]{1,0:T(8,128)(2,1)S(1)}, u32[]{:S(2)}, u32[]{:S(2)}) collective-permute-start(bf16[256,128]{1,0:T(8,128)(2,1)S(1)} %collective-permute-done.refs_1_), channel_id=1, source_target_pairs={{0,6},{1,7},{2,4},{3,5},{4,2},{5,3},{6,0},{7,1},{8,14},{9,15},{10,... | collective-permute-start | bytes 196616 | tf_op jit(solution)/shard_map/ppermute | solution.py:989
  12.8 4.3 %collective-permute-start.7 = (bf16[256,128]{1,0:T(8,128)(2,1)S(1)}, bf16[256,128]{1,0:T(8,128)(2,1)S(1)}, u32[]{:S(2)}, u32[]{:S(2)}) collective-permute-start(bf16[256,128]{1,0:T(8,128)(2,1)S(1)} %collective-permute-done.refs_1_), channel_id=1, source_target_pairs={{0,4},{1,5},{2,6},{3,7},{4,0},{5,1},{6,2},{7,3},{8,12},{9,13},{10,... | collective-permute-start | bytes 196616 | tf_op jit(solution)/shard_map/ppermute | solution.py:989
  13.4 4.3 %collective-permute-start.6 = (bf16[256,128]{1,0:T(8,128)(2,1)S(1)}, bf16[256,128]{1,0:T(8,128)(2,1)S(1)}, u32[]{:S(2)}, u32[]{:S(2)}) collective-permute-start(bf16[256,128]{1,0:T(8,128)(2,1)S(1)} %collective-permute-done.refs_1_), channel_id=1, source_target_pairs={{0,2},{1,3},{2,0},{3,1},{4,6},{5,7},{6,4},{7,5},{8,10},{9,11},{10,... | collective-permute-start | bytes 196616 | tf_op jit(solution)/shard_map/ppermute | solution.py:989
  14.3 3.4 %collective-permute-start.2 = (bf16[256,128]{1,0:T(8,128)(2,1)S(1)}, bf16[256,128]{1,0:T(8,128)(2,1)S(1)}, u32[]{:S(2)}, u32[]{:S(2)}) collective-permute-start(bf16[256,128]{1,0:T(8,128)(2,1)S(1)} %collective-permute-done.refs_1_), channel_id=1, source_target_pairs={{0,1},{1,0},{2,3},{3,2},{4,5},{5,4},{6,7},{7,6},{8,9},{9,8},{10,11... | collective-permute-start | bytes 196616 | tf_op jit(solution)/shard_map/ppermute | solution.py:989
  14.3 1.4 %collective-permute-start.11 = (bf16[256,128]{1,0:T(8,128)(2,1)S(1)}, bf16[256,128]{1,0:T(8,128)(2,1)S(1)}, u32[]{:S(2)}, u32[]{:S(2)}) collective-permute-start(bf16[256,128]{1,0:T(8,128)(2,1)S(1)} %collective-permute-done.5.refs_6_), channel_id=1, source_target_pairs={{0,1},{1,0},{2,3},{3,2},{4,5},{5,4},{6,7},{7,6},{8,9},{9,8},{10,11... | collective-permute-start | bytes 196616 | tf_op jit(solution)/shard_map/ppermute | solution.py:989
  15.7 3.5 %collective-permute-start.10 = (bf16[256,128]{1,0:T(8,128)(2,1)S(1)}, bf16[256,128]{1,0:T(8,128)(2,1)S(1)}, u32[]{:S(2)}, u32[]{:S(2)}) collective-permute-start(bf16[256,128]{1,0:T(8,128)(2,1)S(1)} %collective-permute-done.4.refs_5_), channel_id=1, source_target_pairs={{0,1},{1,0},{2,3},{3,2},{4,5},{5,4},{6,7},{7,6},{8,9},{9,8},{10,11... | collective-permute-start | bytes 196616 | tf_op jit(solution)/shard_map/ppermute | solution.py:989
  16.0 3.2 %collective-permute-start.9 = (bf16[256,128]{1,0:T(8,128)(2,1)S(1)}, bf16[256,128]{1,0:T(8,128)(2,1)S(1)}, u32[]{:S(2)}, u32[]{:S(2)}) collective-permute-start(bf16[256,128]{1,0:T(8,128)(2,1)S(1)} %collective-permute-done.3.refs_4_), channel_id=1, source_target_pairs={{0,1},{1,0},{2,3},{3,2},{4,5},{5,4},{6,7},{7,6},{8,9},{9,8},{10,11... | collective-permute-start | bytes 196616 | tf_op jit(solution)/shard_map/ppermute | solution.py:989
  17.1 2.2 %collective-permute-start.14 = (bf16[256,128]{1,0:T(8,128)(2,1)S(1)}, bf16[256,128]{1,0:T(8,128)(2,1)S(1)}, u32[]{:S(2)}, u32[]{:S(2)}) collective-permute-start(bf16[256,128]{1,0:T(8,128)(2,1)S(1)} %collective-permute-done.8.refs_9_), channel_id=1, source_target_pairs={{0,1},{1,0},{2,3},{3,2},{4,5},{5,4},{6,7},{7,6},{8,9},{9,8},{10,11... | collective-permute-start | bytes 196616 | tf_op jit(solution)/shard_map/ppermute | solution.py:989
  17.7 1.6 %collective-permute-start.13 = (bf16[256,128]{1,0:T(8,128)(2,1)S(1)}, bf16[256,128]{1,0:T(8,128)(2,1)S(1)}, u32[]{:S(2)}, u32[]{:S(2)}) collective-permute-start(bf16[256,128]{1,0:T(8,128)(2,1)S(1)} %collective-permute-done.7.refs_8_), channel_id=1, source_target_pairs={{0,1},{1,0},{2,3},{3,2},{4,5},{5,4},{6,7},{7,6},{8,9},{9,8},{10,11... | collective-permute-start | bytes 196616 | tf_op jit(solution)/shard_map/ppermute | solution.py:989
  17.7 1.6 %collective-permute-start.12 = (bf16[256,128]{1,0:T(8,128)(2,1)S(1)}, bf16[256,128]{1,0:T(8,128)(2,1)S(1)}, u32[]{:S(2)}, u32[]{:S(2)}) collective-permute-start(bf16[256,128]{1,0:T(8,128)(2,1)S(1)} %collective-permute-done.6.refs_7_), channel_id=1, source_target_pairs={{0,1},{1,0},{2,3},{3,2},{4,5},{5,4},{6,7},{7,6},{8,9},{9,8},{10,11... | collective-permute-start | bytes 196616 | tf_op jit(solution)/shard_map/ppermute | solution.py:989
  48.6 1.5 %collective-permute-start.15 = (f16[768,128]{1,0:T(8,128)(2,1)S(1)}, f16[768,128]{1,0:T(8,128)(2,1)S(1)}, u32[]{:S(2)}, u32[]{:S(2)}) collective-permute-start(f16[768,128]{1,0:T(8,128)(2,1)S(1)} %fusion), channel_id=1, source_target_pairs={{0,1},{1,0},{2,3},{3,2},{4,5},{5,4},{6,7},{7,6},{8,9},{9,8},{10,11... | collective-permute-start | bytes 589832 | tf_op jit(solution)/shard_map/ppermute | solution.py:989
  50.3 24.8 %copy-start.2 = (f32[11,128,128]{2,1,0:T(8,128)S(1)}, f32[11,128,128]{2,1,0:T(8,128)}, u32[]{:S(2)}) copy-start(f32[11,128,128]{2,1,0:T(8,128)} %mats_v_ref.1) | copy-start | bytes 2162692
  62.1 13.0 %copy-start = (f32[11,128,128]{2,1,0:T(8,128)S(1)}, f32[11,128,128]{2,1,0:T(8,128)}, u32[]{:S(2)}) copy-start(f32[11,128,128]{2,1,0:T(8,128)} %mats_ref.1) | copy-start | bytes 2162692
  62.2 13.0 %copy-start.1 = (f32[11,128,128]{2,1,0:T(8,128)S(1)}, f32[11,128,128]{2,1,0:T(8,128)}, u32[]{:S(2)}) copy-start(f32[11,128,128]{2,1,0:T(8,128)} %mats_m_ref.1) | copy-start | bytes 2162692
  73.7 1.4 %collective-permute-start.16 = (f16[768,128]{1,0:T(8,128)(2,1)S(1)}, f16[768,128]{1,0:T(8,128)(2,1)S(1)}, u32[]{:S(2)}, u32[]{:S(2)}) collective-permute-start(f16[768,128]{1,0:T(8,128)(2,1)S(1)} %bitcast.27), channel_id=1, source_target_pairs={{0,1},{1,0},{2,3},{3,2},{4,5},{5,4},{6,7},{7,6},{8,9},{9,8},{10,11... | collective-permute-start | bytes 589832 | tf_op jit(solution)/shard_map/ppermute | solution.py:989
